TPU v7x, 128 devices: a whole 4x4x4 slice. The times are simulated.
128 devices in a mesh: rows: 128 (over y, z, x, core).
Axes of the slice: x: 4, y: 4, z: 4, core: 2. Of those that a mesh axis runs over, the one named last changes fastest.
Arguments:
- slab: bfloat16 [262144, 4096], P('rows'), may hold values from -60 to 60, as said below
- test_matrix: bfloat16 [4096, 128], replicated, may hold values from -0.09375 to 0.09375
Outputs:
- projected: float32 [128, 4096], P(None, 'rows')
Inputs may be any that keep to these rules, and one draw needn't show every extreme that they name: Entries of the slab are of order one to some tens.
All inputs are finite; a program needn't handle non-finite values.
Results may differ from a plain program's by a relative error of at most 0.0003.
Values sent between devices are 32-bit elements; how exact they have to be, the bound alone decides.
No kernel may reach another device: no remote copies, remote signals or barrier semaphores. Data moves between devices by JAX's collectives and lax.ppermute only.
A program may use at most 64 MiB of HBM per device.

v0:
```python
import jax
import jax.numpy as jnp
from jax import lax
from jax.sharding import PartitionSpec as P

highest = lax.Precision.HIGHEST


def cholesky_lower(gram_sum):
    order = gram_sum.shape[0]
    places = jnp.arange(order, dtype=jnp.int32)

    def column_step(index, lower):
        unit = (places == index).astype(jnp.float32)
        column = jnp.dot(gram_sum, unit, precision=highest)
        row_of_l = jnp.dot(unit, lower, precision=highest)
        column = column - jnp.dot(lower, row_of_l, precision=highest)
        pivot = jnp.sqrt(jnp.dot(unit, column, precision=highest))
        keep = (places >= index).astype(jnp.float32)
        return lower + jnp.outer(column * keep / pivot, unit)

    return lax.fori_loop(0, order, column_step, jnp.zeros((order, order), jnp.float32))


def invert_lower(lower):
    order = lower.shape[0]
    places = jnp.arange(order, dtype=jnp.int32)

    def row_step(index, inverse):
        unit = (places == index).astype(jnp.float32)
        row_of_l = jnp.dot(unit, lower, precision=highest)
        pivot = jnp.dot(row_of_l, unit, precision=highest)
        below = row_of_l * (places < index).astype(jnp.float32)
        new_row = (unit - jnp.dot(below, inverse, precision=highest)) / pivot
        return inverse + jnp.outer(unit, new_row)

    return lax.fori_loop(0, order, row_step, jnp.zeros((order, order), jnp.float32))


def accumulate(left_side, slab):
    local_rows = slab.shape[0]
    block_rows = min(512, local_rows)
    block_count = local_rows // block_rows
    left_blocks = left_side.reshape(block_count, block_rows, left_side.shape[1])
    slab_blocks = slab.reshape(block_count, block_rows, slab.shape[1])

    def advance(running, entry):
        left_part, slab_part = entry
        return (
            running + jnp.dot(left_part.T, slab_part.astype(jnp.float32), precision=highest),
            None,
        )

    start = jnp.zeros((left_side.shape[1], slab.shape[1]), jnp.float32)
    running, _ = lax.scan(advance, start, (left_blocks, slab_blocks))
    return running


def body(slab, test_matrix):
    sketch = jnp.dot(slab, test_matrix, preferred_element_type=jnp.float32)
    gram_local = jnp.dot(sketch.T, sketch, precision=highest)
    gram_sum = lax.psum(gram_local, "rows")
    inverse_l = invert_lower(cholesky_lower(gram_sum))
    basis_q = jnp.dot(sketch, inverse_l.T, precision=highest)
    projected = lax.psum_scatter(accumulate(basis_q, slab), "rows", scatter_dimension=1, tiled=True)
    return projected


def solution(mesh):
    placed = (P("rows", None), P())
    return jax.shard_map(
        body, mesh=mesh, in_specs=placed, out_specs=P(None, "rows"), check_vma=False
    )
```

profile of v0, /device:TPU:0, one launch (start us, length us, event | category | flops | bytes accessed | tf_op | source)
XLA Modules:
  0.0 1413.1 jit_solution(2447905480849934930)
XLA Ops:
  6.5 1.2 copy-done
  7.8 8.1 fusion.41
  15.9 2.4 fusion.42
  18.4 137.9 %all-reduce.2.cloned.1.call-done = f32[128,128]{1,0:T(8,128)} async-done(((f32[128,128]{1,0:T(8,128)}), f32[128,128]{1,0:T(8,128)}) %all-reduce.2.cloned.1.call-update) | async-done | bytes 65552 | tf_op jit(solution)/shard_map/psum | solution.py:62
  156.3 367.7 %while.42 = (s32[]{:T(128)}, f32[128,128]{1,0:T(8,128)S(1)}, f32[128,128]{1,0:T(8,128)}, s32[]{:T(128)}, s32[]{:T(128)}) while((s32[]{:T(128)}, f32[128,128]{1,0:T(8,128)S(1)}, f32[128,128]{1,0:T(8,128)}, s32[]{:T(128)}, s32[]{:T(128)}) %tuple.88), condition=%wide.region_2.0_spmd.clone.clone, body=%wide.region_1.0_spmd.clone.clone.sunk | while | flops 673154 | bytes 332917 | solution.py:22
  159.2 1.0 convolution_bitcast_fusion.7
  162.1 1.0 convolution_bitcast_fusion.7
  164.9 1.0 convolution_bitcast_fusion.7
  167.8 1.0 convolution_bitcast_fusion.7
  170.7 1.0 convolution_bitcast_fusion.7
  173.6 1.0 convolution_bitcast_fusion.7
  176.4 1.0 convolution_bitcast_fusion.7
  179.3 1.0 convolution_bitcast_fusion.7
  182.2 1.0 convolution_bitcast_fusion.7
  185.0 1.0 convolution_bitcast_fusion.7
  187.9 1.0 convolution_bitcast_fusion.7
  190.8 1.0 convolution_bitcast_fusion.7
  193.7 1.0 convolution_bitcast_fusion.7
  196.5 1.0 convolution_bitcast_fusion.7
  199.4 1.0 convolution_bitcast_fusion.7
  202.3 1.0 convolution_bitcast_fusion.7
  205.2 1.0 convolution_bitcast_fusion.7
  208.0 1.0 convolution_bitcast_fusion.7
  210.9 1.0 convolution_bitcast_fusion.7
  213.8 1.0 convolution_bitcast_fusion.7
  216.7 1.0 convolution_bitcast_fusion.7
  219.5 1.0 convolution_bitcast_fusion.7
  222.4 1.0 convolution_bitcast_fusion.7
  225.3 1.0 convolution_bitcast_fusion.7
  228.1 1.0 convolution_bitcast_fusion.7
  231.0 1.0 convolution_bitcast_fusion.7
  233.9 1.0 convolution_bitcast_fusion.7
  236.8 1.0 convolution_bitcast_fusion.7
  239.6 1.0 convolution_bitcast_fusion.7
  242.5 1.0 convolution_bitcast_fusion.7
  245.4 1.0 convolution_bitcast_fusion.7
  248.3 1.0 convolution_bitcast_fusion.7
  251.1 1.0 convolution_bitcast_fusion.7
  254.0 1.0 convolution_bitcast_fusion.7
  256.9 1.0 convolution_bitcast_fusion.7
  259.8 1.0 convolution_bitcast_fusion.7
  262.6 1.0 convolution_bitcast_fusion.7
  265.5 1.0 convolution_bitcast_fusion.7
  268.4 1.0 convolution_bitcast_fusion.7
  271.2 1.0 convolution_bitcast_fusion.7
  274.1 1.0 convolution_bitcast_fusion.7
  285.6 1.0 convolution_bitcast_fusion.7
  314.3 1.0 convolution_bitcast_fusion.7
  340.2 1.0 convolution_bitcast_fusion.7
  368.9 1.0 convolution_bitcast_fusion.7
  394.8 1.0 convolution_bitcast_fusion.7
  423.5 1.0 convolution_bitcast_fusion.7
  449.4 1.0 convolution_bitcast_fusion.7
  478.1 1.0 convolution_bitcast_fusion.7
  504.0 1.0 convolution_bitcast_fusion.7
  524.1 218.7 %while.43 = (s32[]{:T(128)}, f32[128,128]{1,0:T(8,128)S(1)}, f32[128,128]{1,0:T(8,128)S(1)}, s32[]{:T(128)}, s32[]{:T(128)}) while((s32[]{:T(128)}, f32[128,128]{1,0:T(8,128)S(1)}, f32[128,128]{1,0:T(8,128)S(1)}, s32[]{:T(128)}, s32[]{:T(128)}) %tuple.91), condition=%wide.region_4.0_spmd.clone.clone, body=%wide.region_3.0_spmd.clone.clone.sunk | while | flops 460290 | bytes 265316 | solution.py:37
  742.8 3.2 fusion.43
  746.0 18.9 %while.41 = (s32[]{:T(128)}, f32[128,4096]{1,0:T(8,128)S(1)}, f32[4,512,128]{2,1,0:T(8,128)}, bf16[4,512,4096]{2,1,0:T(8,128)(2,1)}, s32[]{:T(128)}, /*index=5*/s32[]{:T(128)}) while((s32[]{:T(128)}, f32[128,4096]{1,0:T(8,128)S(1)}, f32[4,512,128]{2,1,0:T(8,128)}, bf16[4,512,4096]{2,1,0:T(8,128)(2,1)}, s32[]{:T(128)}, ...), condition=%wide.region_6.7_spmd.clone, body=%wide.region_5.6_spmd.clone.sunk | while | flops 3222274048 | bytes 8652374 | solution.py:55
  746.0 4.7 convolution_add_fusion.2
  750.7 4.7 convolution_add_fusion.2
  755.5 4.7 convolution_add_fusion.2
  760.2 4.7 convolution_add_fusion.2
  764.9 1.9 copy.3
  766.8 639.5 %reduce-scatter.2.cloned.1.call-done = f32[128,32]{0,1:T(8,128)} async-done(((f32[128,4096]{0,1:T(8,128)}), f32[128,32]{0,1:T(8,128)}) %reduce-scatter.2.cloned.1.call-update) | async-done | bytes 16400 | tf_op jit(solution)/shard_map/reduce_scatter | solution.py:65
  (1240 shorter events, 443.1 us)
Async XLA Ops:
  6.5 1.2 copy-start
  6.5 149.8 %all-reduce.2.cloned.1.call-start = ((), (), s32[]{:S(2)}) async-start(), calls=%async_computation.1 | async-start | bytes 131072 | tf_op jit(solution)/shard_map/psum | solution.py:62
  15.9 2.5 copy-start.1
  18.4 1387.9 %reduce-scatter.2.cloned.1.call-start = ((), (), s32[]{:S(2)}) async-start(), calls=%async_computation.2 | async-start | bytes 2113536 | tf_op jit(solution)/shard_map/reduce_scatter | solution.py:65
Sparse Core Ops, SparseCore 0:
  18.5 137.7 all-reduce.1
  766.9 639.3 reduce-scatter.1
where the time goes:
time: 1420 us; the launch traced here: 1410 us
  waiting for transfers between devices  777 us (55%)
  matrix products  498 us (35%)
  loops' own time  95.1 us (7%)
  other arithmetic  25.9 us (2%)
    reduce_scatter x1, waiting for transfers between devices, body(): lax.psum_scatter(accumulate(basis_q, slab), 'rows', scatter_dimension=1,...  639 us
    psum x1, waiting for transfers between devices, body(): gram_sum = lax.psum(gram_local, 'rows')  138 us
    dot_general x128, matrix products, column_step(): column = jnp.dot(gram_sum, unit, precision=highest)  124 us
    dot_general x128, matrix products, column_step(): column = column - jnp.dot(lower, row_of_l, precision=highest)  116 us
    dot_general x128, matrix products, row_step(): new_row = (unit - jnp.dot(below, inverse, precision=highest)) / pivot  101 us
    dot_general x128, matrix products, row_step(): row_of_l = jnp.dot(unit, lower, precision=highest)  99.8 us
    another operation x1, loops' own time, cholesky_lower(): lax.fori_loop(0, order, column_step, jnp.zeros((order, order), jnp.float32))  90.7 us
  transfers between devices with their start and end apart: 2, of which 2 were waited for; matrix products, arithmetic and copies ran while one was open for 0% of the time, Pallas kernels for 0%

commit v1 on v0

v1 whole, which is shorter than its diff:
```python
import functools

import jax
import jax.numpy as jnp
from jax import lax
from jax.experimental import pallas as pl
from jax.experimental.pallas import tpu as pltpu
from jax.sharding import Mesh, PartitionSpec as P

AXES = ("y", "z", "x", "c")
CHIPS = ("y", "z", "x")
K = 128
CHUNK = 256
COLS = 256
NT = (((1,), (1,)), ((), ()))


def sketch_kernel(place_ref, slab_ref, omega_t_ref, gram_ref, mine_ref, other_ref, slab_v, parts, sems):
    rows, width = slab_v.shape
    chunks = rows // CHUNK

    def copy(i):
        at = pl.ds(i * CHUNK, CHUNK)
        return pltpu.make_async_copy(slab_ref.at[at, :], slab_v.at[at, :], sems.at[i])

    for i in range(chunks):
        copy(i).start()
    for i in range(chunks):
        copy(i).wait()
        block = slab_v[pl.ds(i * CHUNK, CHUNK), :]
        sketch_t = lax.dot_general(omega_t_ref[...], block, NT, preferred_element_type=jnp.float32)
        high = sketch_t.astype(jnp.bfloat16)
        low = (sketch_t - high.astype(jnp.float32)).astype(jnp.bfloat16)
        parts[pl.ds(0, K), pl.ds(i * CHUNK, CHUNK)] = high
        parts[pl.ds(K, K), pl.ds(i * CHUNK, CHUNK)] = low
    quad = lax.dot_general(parts[...], parts[...], NT, preferred_element_type=jnp.float32)
    gram_ref[...] = (quad[K:, K:] + (quad[:K, K:] + quad[K:, :K])) + quad[:K, :K]

    core = place_ref[0]
    per_tile = COLS // 64

    def column_tile(n, carry):
        both = jnp.dot(
            parts[...], slab_v[:, pl.ds(pl.multiple_of(n * COLS, COLS), COLS)],
            preferred_element_type=jnp.float32,
        )
        tile = (both[K:, :] + both[:K, :]).T.reshape(per_tile, 2, 32, K)
        at = pl.ds(n * per_tile, per_tile)

        @pl.when(core == 0)
        def _():
            mine_ref[at] = tile[:, 0]
            other_ref[at] = tile[:, 1]

        @pl.when(core == 1)
        def _():
            mine_ref[at] = tile[:, 1]
            other_ref[at] = tile[:, 0]

        return carry

    lax.fori_loop(0, width // COLS, column_tile, 0)


def sketch_call(place, slab, omega_t):
    rows, width = slab.shape
    chips = width // 64
    vmem = pl.BlockSpec(memory_space=pltpu.VMEM)
    half = jax.ShapeDtypeStruct((chips, 32, K), jnp.float32)
    return pl.pallas_call(
        sketch_kernel,
        out_shape=(jax.ShapeDtypeStruct((K, K), jnp.float32), half, half),
        in_specs=[
            pl.BlockSpec(memory_space=pltpu.SMEM),
            pl.BlockSpec(memory_space=pl.ANY),
            vmem,
        ],
        out_specs=(vmem, vmem, vmem),
        scratch_shapes=[
            pltpu.VMEM((rows, width), slab.dtype),
            pltpu.VMEM((2 * K, rows), jnp.bfloat16),
            pltpu.SemaphoreType.DMA((rows // CHUNK,)),
        ],
        compiler_params=pltpu.CompilerParams(vmem_limit_bytes=40 * 2**20),
        cost_estimate=pl.CostEstimate(
            flops=2 * rows * width * 3 * K, bytes_accessed=2 * rows * width, transcendentals=0
        ),
        name="sketch",
    )(place, slab, omega_t)


def reciprocal(value):
    guess = pl.reciprocal(value, approx=True)
    guess = guess * (2.0 - value * guess)
    return guess * (2.0 - value * guess)


def factor_rows(blocks):
    shape = (8, K)
    lane = lax.broadcasted_iota(jnp.int32, shape, 1)
    sublane = lax.broadcasted_iota(jnp.int32, shape, 0)
    blocks = list(blocks)
    count = len(blocks)
    done = []
    for b in range(count):
        first = 8 * b
        inside = (lane >= first) & (lane < first + 8)
        here = blocks[b]
        columns = [jnp.broadcast_to(here[:, first + k : first + k + 1], shape) for k in range(8)]
        entry = {
            (i, k): jnp.broadcast_to(columns[k][i : i + 1, :], shape) for k in range(8) for i in range(k, 8)
        }
        cleared = jnp.where(inside, (lane - first == sublane).astype(jnp.float32), here)
        rows = [jnp.broadcast_to(cleared[k : k + 1, :], shape) for k in range(8)]
        inverse_pivot = []
        lower = {}
        for k in range(8):
            inverse = reciprocal(entry[k, k])
            inverse_pivot.append(inverse)
            for i in range(k + 1, 8):
                lower[i, k] = entry[i, k] * inverse
            for i in range(k + 1, 8):
                for j in range(k + 1, i + 1):
                    entry[i, j] = entry[i, j] - (entry[i, k] * entry[j, k]) * inverse
        for k in range(8):
            for m in range(k):
                rows[k] = rows[k] - lower[k, m] * rows[m]
        result = jnp.zeros(shape, jnp.float32)
        for k in range(8):
            result = jnp.where(sublane == k, rows[k] * lax.rsqrt(entry[k, k]), result)
        done.append(jnp.where(lane <= first + sublane, result, 0.0))
        for i in range(b + 1, count):
            target = blocks[i]
            factors = [jnp.broadcast_to(target[:, first + k : first + k + 1], shape) for k in range(8)]
            target = jnp.where(inside, 0.0, target)
            for k in range(8):
                factor = factors[k]
                for m in range(k):
                    factor = factor - factors[m] * entry[k, m]
                factor = factor * inverse_pivot[k]
                factors[k] = factor
                target = target - factor * rows[k]
            blocks[i] = target
    return done


def factor_kernel(gram_ref, inverse_ref):
    blocks = [gram_ref[pl.ds(8 * b, 8), :] for b in range(K // 8)]
    for b, rows in enumerate(factor_rows(blocks)):
        inverse_ref[pl.ds(8 * b, 8), :] = rows


def factor_call(gram):
    vmem = pl.BlockSpec(memory_space=pltpu.VMEM)
    return pl.pallas_call(
        factor_kernel,
        out_shape=jax.ShapeDtypeStruct((K, K), jnp.float32),
        in_specs=[vmem],
        out_specs=vmem,
        cost_estimate=pl.CostEstimate(flops=10**9, bytes_accessed=2**17, transcendentals=0),
        name="factor",
    )(gram)


def project_kernel(inverse_ref, pieces_ref, out_ref):
    total = jnp.sum(pieces_ref[...], axis=0)
    out_ref[...] = lax.dot_general(
        inverse_ref[...], total, NT, precision=lax.Precision.HIGHEST, preferred_element_type=jnp.float32
    )


def project_call(inverse, pieces):
    vmem = pl.BlockSpec(memory_space=pltpu.VMEM)
    return pl.pallas_call(
        project_kernel,
        out_shape=jax.ShapeDtypeStruct((K, pieces.shape[1]), jnp.float32),
        in_specs=[vmem, vmem],
        out_specs=vmem,
        name="project",
    )(inverse, pieces)


def shift(array, axis, size, by):
    return lax.ppermute(array, axis, [(i, (i + by) % size) for i in range(size)])


def sum_over_rows(gram):
    gram = gram + shift(gram, "c", 2, 1)
    for axis in ("x", "z", "y"):
        gram = (gram + shift(gram, axis, 4, 2)) + (shift(gram, axis, 4, 1) + shift(gram, axis, 4, -1))
    return gram


def body(slab, test_matrix):
    place = lax.axis_index("c").astype(jnp.int32).reshape(1)
    gram, mine, other = sketch_call(place, slab, test_matrix.T)
    half = mine + shift(other, "c", 2, 1)
    pieces = lax.all_to_all(half, CHIPS, 0, 0, tiled=True)
    inverse = factor_call(sum_over_rows(gram))
    return project_call(inverse, pieces)


def solution(mesh):
    grid = Mesh(mesh.devices.reshape(4, 4, 4, 2), AXES)
    return jax.shard_map(
        body, mesh=grid, in_specs=(P(AXES, None), P()), out_specs=P(None, AXES), check_vma=False
    )
```

time: 1420 us -> 85.4 us (0.06)
  waiting for transfers between devices: 777 us -> 22.2 us
  matrix products: 498 us -> 0 us
  loops' own time: 95.1 us -> 0 us
  Pallas kernels: 0 us -> 29.4 us
  starting transfers between devices: 0.04 us -> 27.6 us
  other arithmetic: 25.9 us -> 1.88 us
    reduce_scatter x1 -> x0, waiting for transfers between devices: 639 us -> none  [body(): lax.psum_scatter(accumulate(basis_q, slab), 'rows', scatter_dimension=1,...]
    dot_general x647 -> x0, matrix products: 498 us -> none  [the longest x128 124 us: column_step(): column = jnp.dot(gram_sum, unit, precision=highest)]
    psum x1 -> x0, waiting for transfers between devices: 138 us -> none  [body(): gram_sum = lax.psum(gram_local, 'rows')]
    another operation x3 -> x0, loops' own time: 95.1 us -> none  [the longest x1 90.7 us: cholesky_lower(): lax.fori_loop(0, order, column_step, jnp.zeros((order, order), jnp.float32))]
    pallas_call x0 -> x3, Pallas kernels: none -> 29.4 us  [the longest x1 20.5 us: sketch_call(): pl.pallas_call(sketch_kernel, out_shape=(jax.ShapeDtypeStruct((K, K), jnp...]
    add x256 -> x5, other arithmetic: 24.3 us -> 1.88 us  [the longest x1 1.19 us: body(): half = mine + shift(other, 'c', 2, 1)]
    ppermute x0 -> x11, waiting for transfers between devices: none -> 22.2 us  [shift(): lax.ppermute(array, axis, [(i, (i + by) % size) for i in range(size)])]
    ppermute x0 -> x11, starting transfers between devices: none -> 16.1 us  [shift(): lax.ppermute(array, axis, [(i, (i + by) % size) for i in range(size)])]
  transfers between devices with their start and end apart: 2 -> 12, of which waited for: 2 -> 6; matrix products, arithmetic and copies ran while one was open for 0% -> 2% of each run, Pallas kernels for 0% -> 8%
where the time goes in v1:
time: 85.4 us; the launch traced here: 85.1 us
  Pallas kernels  29.4 us (34%)
  starting transfers between devices  27.6 us (32%)
  waiting for transfers between devices  22.2 us (26%)
  local copies, waits for them, and re-layouts  3.98 us (5%)
  other arithmetic  1.88 us (2%)
    ppermute x11, waiting for transfers between devices, shift(): lax.ppermute(array, axis, [(i, (i + by) % size) for i in range(size)])  22.2 us
    pallas_call x1, Pallas kernels, sketch_call(): pl.pallas_call(sketch_kernel, out_shape=(jax.ShapeDtypeStruct((K, K), jnp...  20.5 us
    ppermute x11, starting transfers between devices, shift(): lax.ppermute(array, axis, [(i, (i + by) % size) for i in range(size)])  16.1 us
    all_to_all x1, starting transfers between devices, body(): pieces = lax.all_to_all(half, CHIPS, 0, 0, tiled=True)  11.5 us
    pallas_call x1, Pallas kernels, factor_call(): pl.pallas_call(factor_kernel, out_shape=jax.ShapeDtypeStruct((K, K), jnp....  6.78 us
    unnamed x3, local copies, waits for them, and re-layouts  2.46 us
    pallas_call x1, Pallas kernels, project_call(): pl.pallas_call(project_kernel, out_shape=jax.ShapeDtypeStruct((K, pieces....  2.17 us
  transfers between devices with their start and end apart: 12, of which 6 were waited for; matrix products, arithmetic and copies ran while one was open for 2% of the time, Pallas kernels for 8%

profile of v1, /device:TPU:0, one launch (start us, length us, event | category | flops | bytes accessed | tf_op | source)
XLA Modules:
  0.0 85.1 jit_solution(301135980326081607)
XLA Ops:
  0.0 1.5 %copy.3 = bf16[4096,128]{0,1:T(8,128)(2,1)S(1)} copy(bf16[4096,128]{1,0:T(8,128)(2,1)} %param.3) | data formatting | bytes 2097152 | tf_op args[1]
  1.5 20.5 %sketch.1 = (f32[128,128]{1,0:T(8,128)S(1)}, f32[64,32,128]{2,1,0:T(8,128)S(1)}, f32[64,32,128]{2,1,0:T(8,128)S(1)}) custom-call(s32[1]{0:T(128)} %bitcast.place_ref, bf16[2048,4096]{1,0:T(8,128)(2,1)} %slab_ref.1, bf16[128,4096]{1,0:T(8,128)(2,1)S(1)} %bitcast.2), custom_call_target="tpu_custom_call" | custom-call | flops 6442450944 | bytes 16777216 | tf_op jit(solution)/shard_map/sketch/pallas_call | solution.py:70
  21.9 0.1 collective-permute-start.10
  22.0 0.5 collective-permute-start
  22.5 2.1 %collective-permute-done.10 = f32[64,32,128]{2,1,0:T(8,128)S(1)} collective-permute-done((f32[64,32,128]{2,1,0:T(8,128)S(1)}, f32[64,32,128]{2,1,0:T(8,128)S(1)}, u32[]{:S(2)}, u32[]{:S(2)}) %collective-permute-start.10) | collective-permute-done | bytes 1048608 | tf_op jit(solution)/shard_map/ppermute | solution.py:184
  24.7 1.2 %add.43 = f32[64,32,128]{2,1,0:T(8,128)} add(f32[64,32,128]{2,1,0:T(8,128)S(1)} %get-tuple-element.9, f32[64,32,128]{2,1,0:T(8,128)S(1)} %collective-permute-done.10) | non-fusion elementwise | flops 262144 | bytes 3145728 | tf_op jit(solution)/shard_map/add | solution.py:197
  25.9 11.5 %all-to-all-start = ((f32[64,32,128]{2,1,0:T(8,128)}), f32[64,32,128]{2,1,0:T(8,128)S(1)}, u32[]{:S(2)}, u32[]{:S(2)}) async-start(f32[64,32,128]{2,1,0:T(8,128)} %add.43), calls=%async_computation | async-start | bytes 2097152 | tf_op jit(solution)/shard_map/all_to_all | solution.py:198
  37.4 0.0 collective-permute-done
  37.4 2.9 %collective-permute-start.3 = (f32[128,128]{1,0:T(8,128)S(1)}, f32[128,128]{1,0:T(8,128)S(1)}, u32[]{:S(2)}, u32[]{:S(2)}) collective-permute-start(f32[128,128]{1,0:T(8,128)S(1)} %add.33), channel_id=1, source_target_pairs={{0,6},{2,0},{4,2},{6,4},{1,7},{3,1},{5,3},{7,5},{8,14},{10,8},{12,... | collective-permute-start | bytes 196616 | tf_op jit(solution)/shard_map/ppermute | solution.py:184
  40.3 0.0 collective-permute-start.2
  40.3 2.3 %collective-permute-start.1 = (f32[128,128]{1,0:T(8,128)S(1)}, f32[128,128]{1,0:T(8,128)S(1)}, u32[]{:S(2)}, u32[]{:S(2)}) collective-permute-start(f32[128,128]{1,0:T(8,128)S(1)} %add.33), channel_id=1, source_target_pairs={{0,4},{2,6},{4,0},{6,2},{1,5},{3,7},{5,1},{7,3},{8,12},{10,14},{12... | collective-permute-start | bytes 196616 | tf_op jit(solution)/shard_map/ppermute | solution.py:184
  42.6 10.0 %collective-permute-done.3 = f32[128,128]{1,0:T(8,128)S(1)} collective-permute-done((f32[128,128]{1,0:T(8,128)S(1)}, f32[128,128]{1,0:T(8,128)S(1)}, u32[]{:S(2)}, u32[]{:S(2)}) %collective-permute-start.3) | collective-permute-done | bytes 65568 | tf_op jit(solution)/shard_map/ppermute | solution.py:184
  52.6 1.2 %collective-permute-done.2 = f32[128,128]{1,0:T(8,128)S(1)} collective-permute-done((f32[128,128]{1,0:T(8,128)S(1)}, f32[128,128]{1,0:T(8,128)S(1)}, u32[]{:S(2)}, u32[]{:S(2)}) %collective-permute-start.2) | collective-permute-done | bytes 65568 | tf_op jit(solution)/shard_map/ppermute | solution.py:184
  53.8 1.0 %collective-permute-done.1 = f32[128,128]{1,0:T(8,128)S(1)} collective-permute-done((f32[128,128]{1,0:T(8,128)S(1)}, f32[128,128]{1,0:T(8,128)S(1)}, u32[]{:S(2)}, u32[]{:S(2)}) %collective-permute-start.1) | collective-permute-done | bytes 65568 | tf_op jit(solution)/shard_map/ppermute | solution.py:184
  54.8 2.7 %collective-permute-start.6 = (f32[128,128]{1,0:T(8,128)S(1)}, f32[128,128]{1,0:T(8,128)S(1)}, u32[]{:S(2)}, u32[]{:S(2)}) collective-permute-start(f32[128,128]{1,0:T(8,128)S(1)} %add_add_fusion.2), channel_id=1, source_target_pairs={{0,24},{8,0},{16,8},{24,16},{1,25},{9,1},{17,9},{25,17},{2,26},{10... | collective-permute-start | bytes 196616 | tf_op jit(solution)/shard_map/ppermute | solution.py:184
  57.5 0.0 collective-permute-start.5
  57.5 2.3 %collective-permute-start.4 = (f32[128,128]{1,0:T(8,128)S(1)}, f32[128,128]{1,0:T(8,128)S(1)}, u32[]{:S(2)}, u32[]{:S(2)}) collective-permute-start(f32[128,128]{1,0:T(8,128)S(1)} %add_add_fusion.2), channel_id=1, source_target_pairs={{0,16},{8,24},{16,0},{24,8},{1,17},{9,25},{17,1},{25,9},{2,18},{10... | collective-permute-start | bytes 196616 | tf_op jit(solution)/shard_map/ppermute | solution.py:184
  59.9 0.0 collective-permute-done.6
  59.9 3.9 %collective-permute-done.5 = f32[128,128]{1,0:T(8,128)S(1)} collective-permute-done((f32[128,128]{1,0:T(8,128)S(1)}, f32[128,128]{1,0:T(8,128)S(1)}, u32[]{:S(2)}, u32[]{:S(2)}) %collective-permute-start.5) | collective-permute-done | bytes 65568 | tf_op jit(solution)/shard_map/ppermute | solution.py:184
  63.7 0.0 collective-permute-done.4
  63.7 3.0 %collective-permute-start.9 = (f32[128,128]{1,0:T(8,128)S(1)}, f32[128,128]{1,0:T(8,128)S(1)}, u32[]{:S(2)}, u32[]{:S(2)}) collective-permute-start(f32[128,128]{1,0:T(8,128)S(1)} %add_add_fusion.1), channel_id=1, source_target_pairs={{0,96},{32,0},{64,32},{96,64},{1,97},{33,1},{65,33},{97,65},{2,98}... | collective-permute-start | bytes 196616 | tf_op jit(solution)/shard_map/ppermute | solution.py:184
  66.8 0.0 collective-permute-start.8
  66.8 2.2 %collective-permute-start.7 = (f32[128,128]{1,0:T(8,128)S(1)}, f32[128,128]{1,0:T(8,128)S(1)}, u32[]{:S(2)}, u32[]{:S(2)}) collective-permute-start(f32[128,128]{1,0:T(8,128)S(1)} %add_add_fusion.1), channel_id=1, source_target_pairs={{0,64},{32,96},{64,0},{96,32},{1,65},{33,97},{65,1},{97,33},{2,66}... | collective-permute-start | bytes 196616 | tf_op jit(solution)/shard_map/ppermute | solution.py:184
  69.0 0.0 collective-permute-done.9
  69.0 4.0 %collective-permute-done.8 = f32[128,128]{1,0:T(8,128)S(1)} collective-permute-done((f32[128,128]{1,0:T(8,128)S(1)}, f32[128,128]{1,0:T(8,128)S(1)}, u32[]{:S(2)}, u32[]{:S(2)}) %collective-permute-start.8) | collective-permute-done | bytes 65568 | tf_op jit(solution)/shard_map/ppermute | solution.py:184
  73.0 0.0 collective-permute-done.7
  73.0 0.6 add_add_fusion.gram_ref
  73.6 6.8 %factor.1.inverse_ref = f32[128,128]{1,0:T(8,128)} custom-call(f32[128,128]{1,0:T(8,128)} %add_add_fusion.gram_ref), custom_call_target="tpu_custom_call" | custom-call | flops 1000000000 | bytes 131072 | tf_op jit(solution)/shard_map/factor/pallas_call | solution.py:155
  80.4 0.0 all-to-all-done.pieces_ref
  80.4 0.0 copy-start
  80.4 1.0 %copy-done = f32[64,32,128]{2,1,0:T(8,128)} copy-done((f32[64,32,128]{2,1,0:T(8,128)}, f32[64,32,128]{2,1,0:T(8,128)S(1)}, u32[]{:S(2)}) %copy-start) | copy-done | bytes 1048600
  81.4 2.2 %project.1 = f32[128,32]{1,0:T(8,128)} custom-call(f32[128,128]{1,0:T(8,128)} %factor.1.inverse_ref, f32[64,32,128]{2,1,0:T(8,128)} %copy-done), custom_call_target="tpu_custom_call" | custom-call | tf_op jit(solution)/shard_map/project/pallas_call | solution.py:174
  83.5 1.5 %copy.4 = f32[128,32]{0,1:T(8,128)} copy(f32[128,32]{1,0:T(8,128)} %project.1) | data formatting | bytes 32768 | tf_op jit(solution)/shard_map/project/pallas_call | solution.py:174
  (3 shorter events, 0.0 us)
Async XLA Ops:
  21.9 2.7 %collective-permute-start.10 = (f32[64,32,128]{2,1,0:T(8,128)S(1)}, f32[64,32,128]{2,1,0:T(8,128)S(1)}, u32[]{:S(2)}, u32[]{:S(2)}) collective-permute-start(f32[64,32,128]{2,1,0:T(8,128)S(1)} %get-tuple-element.10), channel_id=1, source_target_pairs={{0,1},{1,0},{2,3},{3,2},{4,5},{5,4},{6,7},{7,6},{8,9},{9,8},{10,11... | collective-permute-start | bytes 3145736 | tf_op jit(solution)/shard_map/ppermute | solution.py:184
  22.0 15.3 %collective-permute-start = (f32[128,128]{1,0:T(8,128)S(1)}, f32[128,128]{1,0:T(8,128)S(1)}, u32[]{:S(2)}, u32[]{:S(2)}) collective-permute-start(f32[128,128]{1,0:T(8,128)S(1)} %get-tuple-element.8), channel_id=1, source_target_pairs={{0,1},{1,0},{2,3},{3,2},{4,5},{5,4},{6,7},{7,6},{8,9},{9,8},{10,11... | collective-permute-start | bytes 196616 | tf_op jit(solution)/shard_map/ppermute | solution.py:184
  25.9 54.5 %all-to-all-start = ((f32[64,32,128]{2,1,0:T(8,128)}), f32[64,32,128]{2,1,0:T(8,128)S(1)}, u32[]{:S(2)}, u32[]{:S(2)}) async-start(f32[64,32,128]{2,1,0:T(8,128)} %add.43), calls=%async_computation | async-start | bytes 2097152 | tf_op jit(solution)/shard_map/all_to_all | solution.py:198
  37.4 15.2 %collective-permute-start.3 = (f32[128,128]{1,0:T(8,128)S(1)}, f32[128,128]{1,0:T(8,128)S(1)}, u32[]{:S(2)}, u32[]{:S(2)}) collective-permute-start(f32[128,128]{1,0:T(8,128)S(1)} %add.33), channel_id=1, source_target_pairs={{0,6},{2,0},{4,2},{6,4},{1,7},{3,1},{5,3},{7,5},{8,14},{10,8},{12,... | collective-permute-start | bytes 196616 | tf_op jit(solution)/shard_map/ppermute | solution.py:184
  40.3 13.5 %collective-permute-start.2 = (f32[128,128]{1,0:T(8,128)S(1)}, f32[128,128]{1,0:T(8,128)S(1)}, u32[]{:S(2)}, u32[]{:S(2)}) collective-permute-start(f32[128,128]{1,0:T(8,128)S(1)} %add.33), channel_id=1, source_target_pairs={{0,2},{2,4},{4,6},{6,0},{1,3},{3,5},{5,7},{7,1},{8,10},{10,12},{12... | collective-permute-start | bytes 196616 | tf_op jit(solution)/shard_map/ppermute | solution.py:184
  40.3 14.5 %collective-permute-start.1 = (f32[128,128]{1,0:T(8,128)S(1)}, f32[128,128]{1,0:T(8,128)S(1)}, u32[]{:S(2)}, u32[]{:S(2)}) collective-permute-start(f32[128,128]{1,0:T(8,128)S(1)} %add.33), channel_id=1, source_target_pairs={{0,4},{2,6},{4,0},{6,2},{1,5},{3,7},{5,1},{7,3},{8,12},{10,14},{12... | collective-permute-start | bytes 196616 | tf_op jit(solution)/shard_map/ppermute | solution.py:184
  54.8 5.1 %collective-permute-start.6 = (f32[128,128]{1,0:T(8,128)S(1)}, f32[128,128]{1,0:T(8,128)S(1)}, u32[]{:S(2)}, u32[]{:S(2)}) collective-permute-start(f32[128,128]{1,0:T(8,128)S(1)} %add_add_fusion.2), channel_id=1, source_target_pairs={{0,24},{8,0},{16,8},{24,16},{1,25},{9,1},{17,9},{25,17},{2,26},{10... | collective-permute-start | bytes 196616 | tf_op jit(solution)/shard_map/ppermute | solution.py:184
  57.5 6.2 %collective-permute-start.5 = (f32[128,128]{1,0:T(8,128)S(1)}, f32[128,128]{1,0:T(8,128)S(1)}, u32[]{:S(2)}, u32[]{:S(2)}) collective-permute-start(f32[128,128]{1,0:T(8,128)S(1)} %add_add_fusion.2), channel_id=1, source_target_pairs={{0,8},{8,16},{16,24},{24,0},{1,9},{9,17},{17,25},{25,1},{2,10},{10... | collective-permute-start | bytes 196616 | tf_op jit(solution)/shard_map/ppermute | solution.py:184
  57.5 6.2 %collective-permute-start.4 = (f32[128,128]{1,0:T(8,128)S(1)}, f32[128,128]{1,0:T(8,128)S(1)}, u32[]{:S(2)}, u32[]{:S(2)}) collective-permute-start(f32[128,128]{1,0:T(8,128)S(1)} %add_add_fusion.2), channel_id=1, source_target_pairs={{0,16},{8,24},{16,0},{24,8},{1,17},{9,25},{17,1},{25,9},{2,18},{10... | collective-permute-start | bytes 196616 | tf_op jit(solution)/shard_map/ppermute | solution.py:184
  63.7 5.3 %collective-permute-start.9 = (f32[128,128]{1,0:T(8,128)S(1)}, f32[128,128]{1,0:T(8,128)S(1)}, u32[]{:S(2)}, u32[]{:S(2)}) collective-permute-start(f32[128,128]{1,0:T(8,128)S(1)} %add_add_fusion.1), channel_id=1, source_target_pairs={{0,96},{32,0},{64,32},{96,64},{1,97},{33,1},{65,33},{97,65},{2,98}... | collective-permute-start | bytes 196616 | tf_op jit(solution)/shard_map/ppermute | solution.py:184
  66.8 6.2 %collective-permute-start.8 = (f32[128,128]{1,0:T(8,128)S(1)}, f32[128,128]{1,0:T(8,128)S(1)}, u32[]{:S(2)}, u32[]{:S(2)}) collective-permute-start(f32[128,128]{1,0:T(8,128)S(1)} %add_add_fusion.1), channel_id=1, source_target_pairs={{0,32},{32,64},{64,96},{96,0},{1,33},{33,65},{65,97},{97,1},{2,34}... | collective-permute-start | bytes 196616 | tf_op jit(solution)/shard_map/ppermute | solution.py:184
  66.8 6.2 %collective-permute-start.7 = (f32[128,128]{1,0:T(8,128)S(1)}, f32[128,128]{1,0:T(8,128)S(1)}, u32[]{:S(2)}, u32[]{:S(2)}) collective-permute-start(f32[128,128]{1,0:T(8,128)S(1)} %add_add_fusion.1), channel_id=1, source_target_pairs={{0,64},{32,96},{64,0},{96,32},{1,65},{33,97},{65,1},{97,33},{2,66}... | collective-permute-start | bytes 196616 | tf_op jit(solution)/shard_map/ppermute | solution.py:184
  80.4 1.0 %copy-start = (f32[64,32,128]{2,1,0:T(8,128)}, f32[64,32,128]{2,1,0:T(8,128)S(1)}, u32[]{:S(2)}) copy-start(f32[64,32,128]{2,1,0:T(8,128)S(1)} %all-to-all-done.pieces_ref) | copy-start | bytes 3145732

commit v2 on v1

v2 whole, which is shorter than its diff:
```python
import jax
import jax.numpy as jnp
from jax import lax
from jax.experimental import pallas as pl
from jax.experimental.pallas import tpu as pltpu
from jax.sharding import Mesh, PartitionSpec as P

AXES = ("y", "z", "x", "c")
K = 128
CHUNK = 256
AHEAD = 3
COLS = 512
NT = (((1,), (1,)), ((), ()))


def sketch_kernel(place_ref, slab_ref, omega_ref, gram_ref, mine_ref, other_ref, slab_v, omega_v, beside, above, sems, omega_sem):
    rows, width = slab_v.shape
    chunks = rows // CHUNK

    def copy(i):
        at = pl.ds(i * CHUNK, CHUNK)
        return pltpu.make_async_copy(slab_ref.at[at, :], slab_v.at[at, :], sems.at[i])

    def split(value):
        high = value.astype(jnp.bfloat16)
        return high, (value - high.astype(jnp.float32)).astype(jnp.bfloat16)

    omega_copy = pltpu.make_async_copy(omega_ref, omega_v, omega_sem)
    omega_copy.start()
    copy(0).start()
    omega_copy.wait()
    for i in range(1, AHEAD):
        copy(i).start()
    for i in range(chunks):
        copy(i).wait()
        if i + AHEAD < chunks:
            copy(i + AHEAD).start()
        at = pl.ds(i * CHUNK, CHUNK)
        sketch = jnp.dot(slab_v[at, :], omega_v[...], preferred_element_type=jnp.float32)
        beside[at, :K], beside[at, K:] = split(sketch)
        above[:K, at], above[K:, at] = split(sketch.T)
    gram = jnp.dot(above[...], beside[...], preferred_element_type=jnp.float32)
    gram_ref[...] = (gram[K:, K:] + (gram[:K, K:] + gram[K:, :K])) + gram[:K, :K]

    core = place_ref[0]
    groups = COLS // 256
    for n in range(width // COLS):
        both = jnp.dot(above[...], slab_v[:, pl.ds(n * COLS, COLS)], preferred_element_type=jnp.float32)
        tile = (both[K:, :] + both[:K, :]).T.reshape(groups, 4, 2, 32, K)
        at = pl.ds(n * groups, groups)
        for x in range(4):
            even, odd = tile[:, x, 0], tile[:, x, 1]
            mine_ref[x, at] = jnp.where(core == 0, even, odd)
            other_ref[x, at] = jnp.where(core == 0, odd, even)


def sketch_call(place, slab, omega):
    rows, width = slab.shape
    vmem = pl.BlockSpec(memory_space=pltpu.VMEM)
    hbm = pl.BlockSpec(memory_space=pltpu.HBM)
    half = jax.ShapeDtypeStruct((4, width // 256, 32, K), jnp.float32)
    return pl.pallas_call(
        sketch_kernel,
        out_shape=(jax.ShapeDtypeStruct((K, K), jnp.float32), half, half),
        in_specs=[pl.BlockSpec(memory_space=pltpu.SMEM), hbm, hbm],
        out_specs=(vmem,) * 3,
        scratch_shapes=[
            pltpu.VMEM((rows, width), slab.dtype),
            pltpu.VMEM(omega.shape, omega.dtype),
            pltpu.VMEM((rows, 2 * K), jnp.bfloat16),
            pltpu.VMEM((2 * K, rows), jnp.bfloat16),
            pltpu.SemaphoreType.DMA((rows // CHUNK,)),
            pltpu.SemaphoreType.DMA,
        ],
        compiler_params=pltpu.CompilerParams(vmem_limit_bytes=36 * 2**20),
        cost_estimate=pl.CostEstimate(
            flops=2 * rows * width * 3 * K, bytes_accessed=2 * rows * width, transcendentals=0
        ),
        name="sketch",
    )(place, slab, omega)


def factor_rows(blocks):
    shape = (8, K)
    lane = lax.broadcasted_iota(jnp.int32, shape, 1)
    sublane = lax.broadcasted_iota(jnp.int32, shape, 0)
    blocks = list(blocks)
    count = len(blocks)
    done = []

    def column(array, at):
        return jnp.broadcast_to(array[:, at : at + 1], shape)

    def row(array, at):
        return jnp.broadcast_to(array[at : at + 1, :], shape)

    for b in range(count):
        first = 8 * b
        inside = (lane >= first) & (lane < first + 8)
        columns = [column(blocks[b], first + k) for k in range(8)]
        entry = {(i, k): row(columns[k], i) for k in range(8) for i in range(k, 8)}
        cleared = jnp.where(inside, (lane - first == sublane).astype(jnp.float32), blocks[b])
        rows = [row(cleared, k) for k in range(8)]
        inverse = [None] * 8
        lower = {}
        for k in range(8):
            inverse[k] = pltpu.reciprocal(entry[k, k], approx=True)
            for i in range(k + 1, 8):
                lower[i, k] = entry[i, k] * inverse[k]
            for i in range(k + 1, 8):
                for j in range(k + 1, i + 1):
                    entry[i, j] = entry[i, j] - lower[i, k] * entry[j, k]
        for k in range(8):
            for m in range(k):
                rows[k] = rows[k] - lower[k, m] * rows[m]
        result = jnp.zeros(shape, jnp.float32)
        for k in range(8):
            result = jnp.where(sublane == k, rows[k] * lax.rsqrt(entry[k, k]), result)
        done.append(jnp.where(lane <= first + sublane, result, 0.0))
        if b + 1 == count:
            break
        target = blocks[b + 1]
        factors = [column(target, first + k) for k in range(8)]
        target = jnp.where(inside, 0.0, target)
        for k in range(8):
            factor = factors[k] * inverse[k]
            for m in range(k + 1, 8):
                factors[m] = factors[m] - factor * entry[m, k]
            target = target - factor * rows[k]
        blocks[b + 1] = target
        solved = [None] * 8
        for k in reversed(range(8)):
            value = rows[k] * inverse[k]
            for m in range(k + 1, 8):
                value = value - lower[m, k] * solved[m]
            solved[k] = value
        for i in range(b + 2, count):
            products = [column(blocks[i], first + k) * solved[k] for k in range(8)]
            while len(products) > 1:
                products = [products[p] + products[p + 1] for p in range(0, len(products), 2)]
            blocks[i] = jnp.where(inside, 0.0, blocks[i]) - products[0]
    return done


def factor_kernel(gram_ref, inverse_ref):
    blocks = [gram_ref[pl.ds(8 * b, 8), :] for b in range(K // 8)]
    for b, rows in enumerate(factor_rows(blocks)):
        inverse_ref[pl.ds(8 * b, 8), :] = rows


def factor_call(gram):
    vmem = pl.BlockSpec(memory_space=pltpu.VMEM)
    return pl.pallas_call(
        factor_kernel,
        out_shape=jax.ShapeDtypeStruct((K, K), jnp.float32),
        in_specs=[vmem],
        out_specs=vmem,
        compiler_params=pltpu.CompilerParams(vmem_limit_bytes=8 * 2**20),
        cost_estimate=pl.CostEstimate(flops=10**9, bytes_accessed=2**17, transcendentals=0),
        name="factor",
    )(gram)


def project_kernel(inverse_ref, pieces_ref, out_ref):
    total = jnp.sum(pieces_ref[...], axis=0)
    out_ref[...] = lax.dot_general(
        total, inverse_ref[...], NT, precision=lax.Precision.HIGHEST, preferred_element_type=jnp.float32
    )


def project_call(inverse, pieces):
    vmem = pl.BlockSpec(memory_space=pltpu.VMEM)
    return pl.pallas_call(
        project_kernel,
        out_shape=jax.ShapeDtypeStruct((pieces.shape[1], K), jnp.float32),
        in_specs=[vmem, vmem],
        out_specs=vmem,
        compiler_params=pltpu.CompilerParams(vmem_limit_bytes=8 * 2**20),
        name="project",
    )(inverse, pieces)


def shift(array, axis, size, by):
    return lax.ppermute(array, axis, [(i, (i + by) % size) for i in range(size)])


def body(slab, test_matrix):
    place = lax.axis_index("c").astype(jnp.int32).reshape(1)
    slab = pltpu.with_memory_space_constraint(slab, pltpu.HBM)
    test_matrix = pltpu.with_memory_space_constraint(test_matrix, pltpu.HBM)
    gram, mine, other = sketch_call(place, slab, test_matrix)
    gram = gram + shift(gram, "c", 2, 1)
    half = mine + shift(other, "c", 2, 1)
    half, gram = lax.optimization_barrier((half, gram))
    part = jnp.sum(lax.all_to_all(half, "x", 0, 0, tiled=True), axis=0)
    for axis in ("z", "y", "x"):
        ahead, behind, across = (shift(gram, axis, 4, by) for by in (1, -1, 2))
        gram = (gram + across) + (ahead + behind)
    pieces = lax.all_to_all(part, ("y", "z"), 0, 0, tiled=True)
    return project_call(factor_call(gram), pieces).T


def solution(mesh):
    grid = Mesh(mesh.devices.reshape(4, 4, 4, 2), AXES)
    return jax.shard_map(
        body, mesh=grid, in_specs=(P(AXES, None), P()), out_specs=P(None, AXES), check_vma=False
    )
```

time: 85.4 us -> 63.9 us (0.75)
  Pallas kernels: 29.4 us -> 18.3 us
  waiting for transfers between devices: 22.2 us -> 14.8 us
  local copies, waits for them, and re-layouts: 3.98 us -> 0 us
    ppermute x11, waiting for transfers between devices: 22.2 us -> 10.6 us  [shift(): lax.ppermute(array, axis, [(i, (i + by) % size) for i in range(size)])]
    pallas_call x1, Pallas kernels: 20.5 us -> 13.3 us  [sketch_call(): pl.pallas_call(sketch_kernel, out_shape=(jax.ShapeDtypeStruct((K, K), jnp...]
    all_to_all x1 -> x2, waiting for transfers between devices: 0.01 us -> 4.21 us  [the longest x1 4.21 us: body(): pieces = lax.all_to_all(part, ('y', 'z'), 0, 0, tiled=True)]
    pallas_call x1, Pallas kernels: 6.78 us -> 4.2 us  [factor_call(): pl.pallas_call(factor_kernel, out_shape=jax.ShapeDtypeStruct((K, K), jnp....]
    unnamed x3 -> x0, local copies, waits for them, and re-layouts: 2.46 us -> none
    pallas_call x1 -> x0, local copies, waits for them, and re-layouts: 1.52 us -> none  [project_call(): pl.pallas_call(project_kernel, out_shape=jax.ShapeDtypeStruct((K, pieces....]
    pallas_call x1, Pallas kernels: 2.17 us -> 0.82 us  [project_call(): pl.pallas_call(project_kernel, out_shape=jax.ShapeDtypeStruct((pieces.sha...]
    ppermute x11, starting transfers between devices: 16.1 us -> 17.4 us  [shift(): lax.ppermute(array, axis, [(i, (i + by) % size) for i in range(size)])]
  transfers between devices with their start and end apart: 12 -> 13, of which waited for: 6 -> 5; matrix products, arithmetic and copies ran while one was open for 2% -> 1% of each run, Pallas kernels for 8% -> 7%
where the time goes in v2:
time: 63.9 us; the launch traced here: 63.4 us
  starting transfers between devices  28.2 us (44%)
  Pallas kernels  18.3 us (29%)
  waiting for transfers between devices  14.8 us (23%)
  other arithmetic  2.02 us (3%)
    ppermute x11, starting transfers between devices, shift(): lax.ppermute(array, axis, [(i, (i + by) % size) for i in range(size)])  17.4 us
    pallas_call x1, Pallas kernels, sketch_call(): pl.pallas_call(sketch_kernel, out_shape=(jax.ShapeDtypeStruct((K, K), jnp...  13.3 us
    ppermute x11, waiting for transfers between devices, shift(): lax.ppermute(array, axis, [(i, (i + by) % size) for i in range(size)])  10.6 us
    all_to_all x1, starting transfers between devices, body(): pieces = lax.all_to_all(part, ('y', 'z'), 0, 0, tiled=True)  6.45 us
    all_to_all x1, starting transfers between devices, body(): part = jnp.sum(lax.all_to_all(half, 'x', 0, 0, tiled=True), axis=0)  4.37 us
    all_to_all x1, waiting for transfers between devices, body(): pieces = lax.all_to_all(part, ('y', 'z'), 0, 0, tiled=True)  4.21 us
    pallas_call x1, Pallas kernels, factor_call(): pl.pallas_call(factor_kernel, out_shape=jax.ShapeDtypeStruct((K, K), jnp....  4.2 us
  transfers between devices with their start and end apart: 13, of which 5 were waited for; matrix products, arithmetic and copies ran while one was open for 1% of the time, Pallas kernels for 7%

profile of v2, /device:TPU:0, one launch (start us, length us, event | category | flops | bytes accessed | tf_op | source)
XLA Modules:
  0.0 63.4 jit_solution(2430133382744687918)
XLA Ops:
  0.0 13.3 %sketch.1 = (f32[128,128]{1,0:T(8,128)S(1)}, f32[4,16,32,128]{3,2,1,0:T(8,128)S(1)}, f32[4,16,32,128]{3,2,1,0:T(8,128)S(1)}) custom-call(s32[1]{0:T(128)} %bitcast.place_ref, bf16[2048,4096]{1,0:T(8,128)(2,1)} %slab_ref.1, bf16[4096,128]{1,0:T(8,128)(2,1)} %omega_ref.1), custom_call_target="tpu_custom_call" | custom-call | flops 6442450944 | bytes 16777216 | tf_op jit(solution)/shard_map/sketch/pallas_call | solution.py:62
  13.3 0.1 collective-permute-start
  13.4 0.5 collective-permute-start.1
  13.9 2.2 %collective-permute-done.1 = f32[128,128]{1,0:T(8,128)S(1)} collective-permute-done((f32[128,128]{1,0:T(8,128)S(1)}, f32[128,128]{1,0:T(8,128)S(1)}, u32[]{:S(2)}, u32[]{:S(2)}) %collective-permute-start.1) | collective-permute-done | bytes 65568 | tf_op jit(solution)/shard_map/ppermute | solution.py:184
  16.1 0.0 collective-permute-done
  16.1 1.2 %add.33 = f32[4,16,32,128]{3,2,1,0:T(8,128)} add(f32[4,16,32,128]{3,2,1,0:T(8,128)S(1)} %get-tuple-element.10, f32[4,16,32,128]{3,2,1,0:T(8,128)S(1)} %collective-permute-done) | non-fusion elementwise | flops 262144 | bytes 3145728 | tf_op jit(solution)/shard_map/add | solution.py:193
  17.3 4.4 %all-to-all-start = ((f32[4,16,32,128]{3,2,1,0:T(8,128)}), f32[4,16,32,128]{3,2,1,0:T(8,128)S(1)}, u32[]{:S(2)}, u32[]{:S(2)}) async-start(f32[4,16,32,128]{3,2,1,0:T(8,128)} %add.33), calls=%async_computation | async-start | bytes 2097152 | tf_op jit(solution)/shard_map/all_to_all | solution.py:195
  21.7 4.0 %collective-permute-start.4 = (f32[128,128]{1,0:T(8,128)S(1)}, f32[128,128]{1,0:T(8,128)S(1)}, u32[]{:S(2)}, u32[]{:S(2)}) collective-permute-start(f32[128,128]{1,0:T(8,128)S(1)} %add.34), channel_id=1, source_target_pairs={{0,24},{8,0},{16,8},{24,16},{1,25},{9,1},{17,9},{25,17},{2,26},{10... | collective-permute-start | bytes 196616 | tf_op jit(solution)/shard_map/ppermute | solution.py:184
  25.7 0.0 collective-permute-start.3
  25.7 1.9 %collective-permute-start.2 = (f32[128,128]{1,0:T(8,128)S(1)}, f32[128,128]{1,0:T(8,128)S(1)}, u32[]{:S(2)}, u32[]{:S(2)}) collective-permute-start(f32[128,128]{1,0:T(8,128)S(1)} %add.34), channel_id=1, source_target_pairs={{0,16},{8,24},{16,0},{24,8},{1,17},{9,25},{17,1},{25,9},{2,18},{10... | collective-permute-start | bytes 196616 | tf_op jit(solution)/shard_map/ppermute | solution.py:184
  27.6 0.0 collective-permute-done.4
  27.6 4.3 %collective-permute-done.3 = f32[128,128]{1,0:T(8,128)S(1)} collective-permute-done((f32[128,128]{1,0:T(8,128)S(1)}, f32[128,128]{1,0:T(8,128)S(1)}, u32[]{:S(2)}, u32[]{:S(2)}) %collective-permute-start.3) | collective-permute-done | bytes 65568 | tf_op jit(solution)/shard_map/ppermute | solution.py:184
  32.0 0.0 collective-permute-done.2
  32.0 3.1 %collective-permute-start.7 = (f32[128,128]{1,0:T(8,128)S(1)}, f32[128,128]{1,0:T(8,128)S(1)}, u32[]{:S(2)}, u32[]{:S(2)}) collective-permute-start(f32[128,128]{1,0:T(8,128)S(1)} %add_add_fusion.2), channel_id=1, source_target_pairs={{0,96},{32,0},{64,32},{96,64},{1,97},{33,1},{65,33},{97,65},{2,98}... | collective-permute-start | bytes 196616 | tf_op jit(solution)/shard_map/ppermute | solution.py:184
  35.1 0.0 collective-permute-start.6
  35.1 2.2 %collective-permute-start.5 = (f32[128,128]{1,0:T(8,128)S(1)}, f32[128,128]{1,0:T(8,128)S(1)}, u32[]{:S(2)}, u32[]{:S(2)}) collective-permute-start(f32[128,128]{1,0:T(8,128)S(1)} %add_add_fusion.2), channel_id=1, source_target_pairs={{0,64},{32,96},{64,0},{96,32},{1,65},{33,97},{65,1},{97,33},{2,66}... | collective-permute-start | bytes 196616 | tf_op jit(solution)/shard_map/ppermute | solution.py:184
  37.3 0.3 collective-permute-done.7
  37.6 3.7 %collective-permute-done.6 = f32[128,128]{1,0:T(8,128)S(1)} collective-permute-done((f32[128,128]{1,0:T(8,128)S(1)}, f32[128,128]{1,0:T(8,128)S(1)}, u32[]{:S(2)}, u32[]{:S(2)}) %collective-permute-start.6) | collective-permute-done | bytes 65568 | tf_op jit(solution)/shard_map/ppermute | solution.py:184
  41.2 0.0 collective-permute-done.5
  41.3 3.3 %collective-permute-start.10 = (f32[128,128]{1,0:T(8,128)S(1)}, f32[128,128]{1,0:T(8,128)S(1)}, u32[]{:S(2)}, u32[]{:S(2)}) collective-permute-start(f32[128,128]{1,0:T(8,128)S(1)} %add_add_fusion.1), channel_id=1, source_target_pairs={{0,6},{2,0},{4,2},{6,4},{1,7},{3,1},{5,3},{7,5},{8,14},{10,8},{12,... | collective-permute-start | bytes 196616 | tf_op jit(solution)/shard_map/ppermute | solution.py:184
  44.5 0.0 collective-permute-start.9
  44.5 2.3 %collective-permute-start.8 = (f32[128,128]{1,0:T(8,128)S(1)}, f32[128,128]{1,0:T(8,128)S(1)}, u32[]{:S(2)}, u32[]{:S(2)}) collective-permute-start(f32[128,128]{1,0:T(8,128)S(1)} %add_add_fusion.1), channel_id=1, source_target_pairs={{0,4},{2,6},{4,0},{6,2},{1,5},{3,7},{5,1},{7,3},{8,12},{10,14},{12... | collective-permute-start | bytes 196616 | tf_op jit(solution)/shard_map/ppermute | solution.py:184
  46.9 0.0 all-to-all-done
  46.9 0.8 %reduce_sum.9 = f32[16,32,128]{2,1,0:T(8,128)} reduce(f32[4,16,32,128]{3,2,1,0:T(8,128)S(1)} %all-to-all-done, f32[]{:T(128)} %constant.1.clone.1), dimensions={0}, to_apply=%region_0.0 | reduce | flops 196608 | bytes 1310724 | tf_op jit(solution)/shard_map/reduce_sum | solution.py:195
  47.6 6.5 %all-to-all-start.1 = ((f32[16,32,128]{2,1,0:T(8,128)}), f32[16,32,128]{2,1,0:T(8,128)S(1)}, u32[]{:S(2)}, u32[]{:S(2)}) async-start(f32[16,32,128]{2,1,0:T(8,128)} %reduce_sum.9), calls=%async_computation.1 | async-start | bytes 524288 | tf_op jit(solution)/shard_map/all_to_all | solution.py:199
  54.1 0.0 collective-permute-done.10
  54.1 0.0 collective-permute-done.9
  54.1 0.0 collective-permute-done.8
  54.2 4.2 %factor.1.inverse_ref = f32[128,128]{1,0:T(8,128)S(1)} custom-call(f32[128,128]{1,0:T(8,128)S(1)} %add_add_fusion.gram_ref), custom_call_target="tpu_custom_call" | custom-call | flops 1000000000 | bytes 131072 | tf_op jit(solution)/shard_map/factor/pallas_call | solution.py:153
  58.4 4.2 %all-to-all-done.1.pieces_ref = f32[16,32,128]{2,1,0:T(8,128)S(1)} async-done(((f32[16,32,128]{2,1,0:T(8,128)}), f32[16,32,128]{2,1,0:T(8,128)S(1)}, u32[]{:S(2)}, u32[]{:S(2)}) %all-to-all-start.1) | async-done | bytes 262176 | tf_op jit(solution)/shard_map/all_to_all | solution.py:199
  62.6 0.8 %project.1 = f32[32,128]{1,0:T(8,128)} custom-call(f32[128,128]{1,0:T(8,128)S(1)} %factor.1.inverse_ref, f32[16,32,128]{2,1,0:T(8,128)S(1)} %all-to-all-done.1.pieces_ref), custom_call_target="tpu_custom_call" | custom-call | tf_op jit(solution)/shard_map/project/pallas_call | solution.py:173
  (4 shorter events, 0.1 us)
Async XLA Ops:
  13.3 2.8 %collective-permute-start = (f32[4,16,32,128]{3,2,1,0:T(8,128)S(1)}, f32[4,16,32,128]{3,2,1,0:T(8,128)S(1)}, u32[]{:S(2)}, u32[]{:S(2)}) collective-permute-start(f32[4,16,32,128]{3,2,1,0:T(8,128)S(1)} %get-tuple-element.11), channel_id=1, source_target_pairs={{0,1},{1,0},{2,3},{3,2},{4,5},{5,4},{6,7},{7,6},{8,9},{9,8},{10,11... | collective-permute-start | bytes 3145736 | tf_op jit(solution)/shard_map/ppermute | solution.py:184
  13.4 2.7 %collective-permute-start.1 = (f32[128,128]{1,0:T(8,128)S(1)}, f32[128,128]{1,0:T(8,128)S(1)}, u32[]{:S(2)}, u32[]{:S(2)}) collective-permute-start(f32[128,128]{1,0:T(8,128)S(1)} %get-tuple-element.12), channel_id=1, source_target_pairs={{0,1},{1,0},{2,3},{3,2},{4,5},{5,4},{6,7},{7,6},{8,9},{9,8},{10,11... | collective-permute-start | bytes 196616 | tf_op jit(solution)/shard_map/ppermute | solution.py:184
  17.3 29.5 %all-to-all-start = ((f32[4,16,32,128]{3,2,1,0:T(8,128)}), f32[4,16,32,128]{3,2,1,0:T(8,128)S(1)}, u32[]{:S(2)}, u32[]{:S(2)}) async-start(f32[4,16,32,128]{3,2,1,0:T(8,128)} %add.33), calls=%async_computation | async-start | bytes 2097152 | tf_op jit(solution)/shard_map/all_to_all | solution.py:195
  21.7 6.0 %collective-permute-start.4 = (f32[128,128]{1,0:T(8,128)S(1)}, f32[128,128]{1,0:T(8,128)S(1)}, u32[]{:S(2)}, u32[]{:S(2)}) collective-permute-start(f32[128,128]{1,0:T(8,128)S(1)} %add.34), channel_id=1, source_target_pairs={{0,24},{8,0},{16,8},{24,16},{1,25},{9,1},{17,9},{25,17},{2,26},{10... | collective-permute-start | bytes 196616 | tf_op jit(solution)/shard_map/ppermute | solution.py:184
  25.7 6.2 %collective-permute-start.3 = (f32[128,128]{1,0:T(8,128)S(1)}, f32[128,128]{1,0:T(8,128)S(1)}, u32[]{:S(2)}, u32[]{:S(2)}) collective-permute-start(f32[128,128]{1,0:T(8,128)S(1)} %add.34), channel_id=1, source_target_pairs={{0,8},{8,16},{16,24},{24,0},{1,9},{9,17},{17,25},{25,1},{2,10},{10... | collective-permute-start | bytes 196616 | tf_op jit(solution)/shard_map/ppermute | solution.py:184
  25.7 6.2 %collective-permute-start.2 = (f32[128,128]{1,0:T(8,128)S(1)}, f32[128,128]{1,0:T(8,128)S(1)}, u32[]{:S(2)}, u32[]{:S(2)}) collective-permute-start(f32[128,128]{1,0:T(8,128)S(1)} %add.34), channel_id=1, source_target_pairs={{0,16},{8,24},{16,0},{24,8},{1,17},{9,25},{17,1},{25,9},{2,18},{10... | collective-permute-start | bytes 196616 | tf_op jit(solution)/shard_map/ppermute | solution.py:184
  32.0 5.6 %collective-permute-start.7 = (f32[128,128]{1,0:T(8,128)S(1)}, f32[128,128]{1,0:T(8,128)S(1)}, u32[]{:S(2)}, u32[]{:S(2)}) collective-permute-start(f32[128,128]{1,0:T(8,128)S(1)} %add_add_fusion.2), channel_id=1, source_target_pairs={{0,96},{32,0},{64,32},{96,64},{1,97},{33,1},{65,33},{97,65},{2,98}... | collective-permute-start | bytes 196616 | tf_op jit(solution)/shard_map/ppermute | solution.py:184
  35.1 6.2 %collective-permute-start.6 = (f32[128,128]{1,0:T(8,128)S(1)}, f32[128,128]{1,0:T(8,128)S(1)}, u32[]{:S(2)}, u32[]{:S(2)}) collective-permute-start(f32[128,128]{1,0:T(8,128)S(1)} %add_add_fusion.2), channel_id=1, source_target_pairs={{0,32},{32,64},{64,96},{96,0},{1,33},{33,65},{65,97},{97,1},{2,34}... | collective-permute-start | bytes 196616 | tf_op jit(solution)/shard_map/ppermute | solution.py:184
  35.1 6.2 %collective-permute-start.5 = (f32[128,128]{1,0:T(8,128)S(1)}, f32[128,128]{1,0:T(8,128)S(1)}, u32[]{:S(2)}, u32[]{:S(2)}) collective-permute-start(f32[128,128]{1,0:T(8,128)S(1)} %add_add_fusion.2), channel_id=1, source_target_pairs={{0,64},{32,96},{64,0},{96,32},{1,65},{33,97},{65,1},{97,33},{2,66}... | collective-permute-start | bytes 196616 | tf_op jit(solution)/shard_map/ppermute | solution.py:184
  41.3 12.8 %collective-permute-start.10 = (f32[128,128]{1,0:T(8,128)S(1)}, f32[128,128]{1,0:T(8,128)S(1)}, u32[]{:S(2)}, u32[]{:S(2)}) collective-permute-start(f32[128,128]{1,0:T(8,128)S(1)} %add_add_fusion.1), channel_id=1, source_target_pairs={{0,6},{2,0},{4,2},{6,4},{1,7},{3,1},{5,3},{7,5},{8,14},{10,8},{12,... | collective-permute-start | bytes 196616 | tf_op jit(solution)/shard_map/ppermute | solution.py:184
  44.5 9.6 %collective-permute-start.9 = (f32[128,128]{1,0:T(8,128)S(1)}, f32[128,128]{1,0:T(8,128)S(1)}, u32[]{:S(2)}, u32[]{:S(2)}) collective-permute-start(f32[128,128]{1,0:T(8,128)S(1)} %add_add_fusion.1), channel_id=1, source_target_pairs={{0,2},{2,4},{4,6},{6,0},{1,3},{3,5},{5,7},{7,1},{8,10},{10,12},{12... | collective-permute-start | bytes 196616 | tf_op jit(solution)/shard_map/ppermute | solution.py:184
  44.5 9.6 %collective-permute-start.8 = (f32[128,128]{1,0:T(8,128)S(1)}, f32[128,128]{1,0:T(8,128)S(1)}, u32[]{:S(2)}, u32[]{:S(2)}) collective-permute-start(f32[128,128]{1,0:T(8,128)S(1)} %add_add_fusion.1), channel_id=1, source_target_pairs={{0,4},{2,6},{4,0},{6,2},{1,5},{3,7},{5,1},{7,3},{8,12},{10,14},{12... | collective-permute-start | bytes 196616 | tf_op jit(solution)/shard_map/ppermute | solution.py:184
  47.6 14.9 %all-to-all-start.1 = ((f32[16,32,128]{2,1,0:T(8,128)}), f32[16,32,128]{2,1,0:T(8,128)S(1)}, u32[]{:S(2)}, u32[]{:S(2)}) async-start(f32[16,32,128]{2,1,0:T(8,128)} %reduce_sum.9), calls=%async_computation.1 | async-start | bytes 524288 | tf_op jit(solution)/shard_map/all_to_all | solution.py:199

commit v3 on v2

--- a/solution.py
+++ b/solution.py
@@ -3,14 +3,27 @@
 from jax import lax
 from jax.experimental import pallas as pl
 from jax.experimental.pallas import tpu as pltpu
-from jax.sharding import Mesh, PartitionSpec as P
-
-AXES = ("y", "z", "x", "c")
+from jax.sharding import PartitionSpec as P
+
+SIDE = 4
 K = 128
 CHUNK = 256
 AHEAD = 3
 COLS = 512
 NT = (((1,), (1,)), ((), ()))
+
+
+def place_of(chip):
+    return chip // SIDE**2, chip // SIDE % SIDE, chip % SIDE
+
+
+def turn(target, here):
+    apart = target ^ here
+    return 2 * ((apart >> 1) ^ (apart & 1)) + (apart >> 1)
+
+
+def device(y, z, x, core):
+    return ((y * SIDE + z) * SIDE + x) * 2 + core
 
 
 def sketch_kernel(place_ref, slab_ref, omega_ref, gram_ref, mine_ref, other_ref, slab_v, omega_v, beside, above, sems, omega_sem):
@@ -42,23 +55,26 @@
     gram = jnp.dot(above[...], beside[...], preferred_element_type=jnp.float32)
     gram_ref[...] = (gram[K:, K:] + (gram[:K, K:] + gram[K:, :K])) + gram[:K, :K]
 
-    core = place_ref[0]
-    groups = COLS // 256
+    y, z, x, core = (place_ref[i] for i in range(4))
+    first = core == 0
     for n in range(width // COLS):
         both = jnp.dot(above[...], slab_v[:, pl.ds(n * COLS, COLS)], preferred_element_type=jnp.float32)
-        tile = (both[K:, :] + both[:K, :]).T.reshape(groups, 4, 2, 32, K)
-        at = pl.ds(n * groups, groups)
-        for x in range(4):
-            even, odd = tile[:, x, 0], tile[:, x, 1]
-            mine_ref[x, at] = jnp.where(core == 0, even, odd)
-            other_ref[x, at] = jnp.where(core == 0, odd, even)
+        tile = (both[K:, :] + both[:K, :]).T.reshape(COLS // 64, 2, 32, K)
+        for chip in range(COLS // 64):
+            to_y, to_z, to_x = place_of(n * (COLS // 64) + chip)
+            even, odd = tile[chip, 0], tile[chip, 1]
+            by_y, by_z, by_x = turn(to_y, y), turn(to_z, z), turn(to_x, x)
+            mine_at = jnp.where(first, by_x, by_z), SIDE * jnp.where(first, by_z, by_x) + by_y
+            other_at = jnp.where(first, by_z, by_x), SIDE * jnp.where(first, by_x, by_z) + by_y
+            mine_ref[mine_at[0], mine_at[1]] = jnp.where(first, even, odd)
+            other_ref[other_at[0], other_at[1]] = jnp.where(first, odd, even)
 
 
 def sketch_call(place, slab, omega):
     rows, width = slab.shape
     vmem = pl.BlockSpec(memory_space=pltpu.VMEM)
     hbm = pl.BlockSpec(memory_space=pltpu.HBM)
-    half = jax.ShapeDtypeStruct((4, width // 256, 32, K), jnp.float32)
+    half = jax.ShapeDtypeStruct((SIDE, SIDE * SIDE, 32, K), jnp.float32)
     return pl.pallas_call(
         sketch_kernel,
         out_shape=(jax.ShapeDtypeStruct((K, K), jnp.float32), half, half),
@@ -156,7 +172,7 @@
         in_specs=[vmem],
         out_specs=vmem,
         compiler_params=pltpu.CompilerParams(vmem_limit_bytes=8 * 2**20),
-        cost_estimate=pl.CostEstimate(flops=10**9, bytes_accessed=2**17, transcendentals=0),
+        cost_estimate=pl.CostEstimate(flops=5 * 10**10, bytes_accessed=2**17, transcendentals=0),
         name="factor",
     )(gram)
 
@@ -180,28 +196,44 @@
     )(inverse, pieces)
 
 
-def shift(array, axis, size, by):
-    return lax.ppermute(array, axis, [(i, (i + by) % size) for i in range(size)])
+def swap_cores(array):
+    return lax.ppermute(array, "rows", [(i, i ^ 1) for i in range(2 * SIDE**3)])
+
+
+def swap_chips(array, axes, mask):
+    pairs = []
+    for chip in range(SIDE**3):
+        for core in range(2):
+            target = list(place_of(chip))
+            target[axes[core]] ^= mask
+            pairs.append((2 * chip + core, device(*target, core)))
+    return lax.ppermute(array, "rows", pairs)
 
 
 def body(slab, test_matrix):
-    place = lax.axis_index("c").astype(jnp.int32).reshape(1)
+    me = lax.axis_index("rows").astype(jnp.int32)
+    place = jnp.stack([*place_of(me // 2), me % 2])
     slab = pltpu.with_memory_space_constraint(slab, pltpu.HBM)
     test_matrix = pltpu.with_memory_space_constraint(test_matrix, pltpu.HBM)
     gram, mine, other = sketch_call(place, slab, test_matrix)
-    gram = gram + shift(gram, "c", 2, 1)
-    half = mine + shift(other, "c", 2, 1)
-    half, gram = lax.optimization_barrier((half, gram))
-    part = jnp.sum(lax.all_to_all(half, "x", 0, 0, tiled=True), axis=0)
-    for axis in ("z", "y", "x"):
-        ahead, behind, across = (shift(gram, axis, 4, by) for by in (1, -1, 2))
-        gram = (gram + across) + (ahead + behind)
-    pieces = lax.all_to_all(part, ("y", "z"), 0, 0, tiled=True)
-    return project_call(factor_call(gram), pieces).T
+
+    pieces = SIDE**3
+    mine, other = mine.reshape(pieces, 32, K), other.reshape(pieces, 32, K)
+    gram = gram.reshape(-1, 32, K)
+    got = swap_cores(jnp.concatenate([other, gram]))
+    part, gram = mine + got[:pieces], gram + got[pieces:]
+    for axes in ((2, 1), (1, 2), (0, 0)):
+        pieces //= 4
+        quarters = [part[i * pieces : (i + 1) * pieces] for i in range(4)]
+        got = [
+            swap_chips(jnp.concatenate([quarters[i], gram]), axes, mask) for i, mask in ((3, 2), (1, 3), (2, 1))
+        ]
+        part = (quarters[0] + got[0][:pieces]) + (got[1][:pieces] + got[2][:pieces])
+        gram = (gram + got[0][pieces:]) + (got[1][pieces:] + got[2][pieces:])
+    return project_call(factor_call(gram.reshape(K, K)), part).T
 
 
 def solution(mesh):
-    grid = Mesh(mesh.devices.reshape(4, 4, 4, 2), AXES)
     return jax.shard_map(
-        body, mesh=grid, in_specs=(P(AXES, None), P()), out_specs=P(None, AXES), check_vma=False
+        body, mesh=mesh, in_specs=(P("rows", None), P()), out_specs=P(None, "rows"), check_vma=False
     )

time: 63.9 us -> 54.1 us (0.85)
  starting transfers between devices: 28.2 us -> 13.7 us
  waiting for transfers between devices: 14.8 us -> 20.5 us
  other arithmetic: 2.02 us -> 0.73 us
    all_to_all x2 -> x0, starting transfers between devices: 10.8 us -> none  [the longest x1 6.45 us: body(): pieces = lax.all_to_all(part, ('y', 'z'), 0, 0, tiled=True)]
    ppermute x11 -> x10, waiting for transfers between devices: 10.6 us -> 20.5 us  [the longest x9 17.8 us: swap_chips(): return lax.ppermute(array, 'rows', pairs)]
    all_to_all x2 -> x0, waiting for transfers between devices: 4.21 us -> none  [the longest x1 4.21 us: body(): pieces = lax.all_to_all(part, ('y', 'z'), 0, 0, tiled=True)]
    ppermute x11 -> x10, starting transfers between devices: 17.4 us -> 13.7 us  [the longest x9 13.6 us: swap_chips(): return lax.ppermute(array, 'rows', pairs)]
    add x5 -> x6, other arithmetic: 1.24 us -> 0.4 us  [the longest x2 0.24 us: body(): part, gram = (mine + got[:pieces], gram + got[pieces:])]
    reduce_sum x1 -> x0, other arithmetic: 0.78 us -> none  [body(): part = jnp.sum(lax.all_to_all(half, 'x', 0, 0, tiled=True), axis=0)]
  transfers between devices with their start and end apart: 13 -> 10, of which waited for: 5 -> 8; matrix products, arithmetic and copies ran while one was open for 1% -> 0% of each run, Pallas kernels for 7% -> 0%
where the time goes in v3:
time: 54.1 us; the launch traced here: 54 us
  waiting for transfers between devices  20.5 us (38%)
  Pallas kernels  18.8 us (35%)
  starting transfers between devices  13.7 us (25%)
  other arithmetic  0.73 us (1%)
    ppermute x9, waiting for transfers between devices, swap_chips(): return lax.ppermute(array, 'rows', pairs)  17.8 us
    pallas_call x1, Pallas kernels, sketch_call(): pl.pallas_call(sketch_kernel, out_shape=(jax.ShapeDtypeStruct((K, K), jnp...  13.8 us
    ppermute x9, starting transfers between devices, swap_chips(): return lax.ppermute(array, 'rows', pairs)  13.6 us
    pallas_call x1, Pallas kernels, factor_call(): pl.pallas_call(factor_kernel, out_shape=jax.ShapeDtypeStruct((K, K), jnp....  4.2 us
    ppermute x1, waiting for transfers between devices, swap_cores(): lax.ppermute(array, 'rows', [(i, i ^ 1) for i in range(2 * SIDE ** 3)])  2.74 us
  transfers between devices with their start and end apart: 10, of which 8 were waited for; matrix products, arithmetic and copies ran while one was open for 0% of the time, Pallas kernels for 0%

profile of v3, /device:TPU:0, one launch (start us, length us, event | category | flops | bytes accessed | tf_op | source)
XLA Modules:
  0.0 54.0 jit_solution(8478660687863752859)
XLA Ops:
  0.0 0.1 pad_add_fusion.place_ref
  0.1 13.8 %sketch.1 = (f32[128,128]{1,0:T(8,128)S(1)}, f32[4,16,32,128]{3,2,1,0:T(8,128)S(1)}, f32[4,16,32,128]{3,2,1,0:T(8,128)S(1)}) custom-call(s32[4]{0:T(128)S(1)} %pad_add_fusion.place_ref, bf16[2048,4096]{1,0:T(8,128)(2,1)} %slab_ref.1, bf16[4096,128]{1,0:T(8,128)(2,1)} %omega_ref.1), custom_call_target="tpu_custom_call" | custom-call | flops 6442450944 | bytes 16777216 | tf_op jit(solution)/shard_map/sketch/pallas_call | solution.py:78
  13.9 0.1 pad_maximum_fusion
  14.0 0.1 collective-permute-start
  14.1 2.7 %collective-permute-done = f32[68,32,128]{2,1,0:T(8,128)S(1)} collective-permute-done((f32[68,32,128]{2,1,0:T(8,128)S(1)}, f32[68,32,128]{2,1,0:T(8,128)S(1)}, u32[]{:S(2)}, u32[]{:S(2)}) %collective-permute-start) | collective-permute-done | bytes 1114144 | tf_op jit(solution)/shard_map/ppermute | solution.py:200
  16.8 0.2 slice_add_fusion
  17.1 0.1 fusion.6
  17.1 0.1 pad_maximum_fusion.3
  17.2 3.2 %collective-permute-start.1 = (f32[20,32,128]{2,1,0:T(8,128)S(1)}, f32[20,32,128]{2,1,0:T(8,128)S(1)}, u32[]{:S(2)}, u32[]{:S(2)}) collective-permute-start(f32[20,32,128]{2,1,0:T(8,128)S(1)} %get-tuple-element.28), channel_id=1, source_target_pairs={{0,4},{1,17},{2,6},{3,19},{4,0},{5,21},{6,2},{7,23},{8,12},{9,25},... | collective-permute-start | bytes 983048 | tf_op jit(solution)/shard_map/ppermute | solution.py:210
  20.4 1.1 %collective-permute-start.2 = (f32[20,32,128]{2,1,0:T(8,128)S(1)}, f32[20,32,128]{2,1,0:T(8,128)S(1)}, u32[]{:S(2)}, u32[]{:S(2)}) collective-permute-start(f32[20,32,128]{2,1,0:T(8,128)S(1)} %get-tuple-element.29), channel_id=1, source_target_pairs={{0,6},{1,25},{2,4},{3,27},{4,2},{5,29},{6,0},{7,31},{8,14},{9,17},... | collective-permute-start | bytes 983048 | tf_op jit(solution)/shard_map/ppermute | solution.py:210
  21.6 0.0 collective-permute-start.3
  21.6 4.4 %collective-permute-done.1 = f32[20,32,128]{2,1,0:T(8,128)S(1)} collective-permute-done((f32[20,32,128]{2,1,0:T(8,128)S(1)}, f32[20,32,128]{2,1,0:T(8,128)S(1)}, u32[]{:S(2)}, u32[]{:S(2)}) %collective-permute-start.1) | collective-permute-done | bytes 327712 | tf_op jit(solution)/shard_map/ppermute | solution.py:210
  26.0 3.4 %collective-permute-done.2 = f32[20,32,128]{2,1,0:T(8,128)S(1)} collective-permute-done((f32[20,32,128]{2,1,0:T(8,128)S(1)}, f32[20,32,128]{2,1,0:T(8,128)S(1)}, u32[]{:S(2)}, u32[]{:S(2)}) %collective-permute-start.2) | collective-permute-done | bytes 327712 | tf_op jit(solution)/shard_map/ppermute | solution.py:210
  29.4 0.2 collective-permute-done.3
  29.6 0.1 fusion
  29.8 4.0 %collective-permute-start.4 = (f32[8,32,128]{2,1,0:T(8,128)S(1)}, f32[8,32,128]{2,1,0:T(8,128)S(1)}, u32[]{:S(2)}, u32[]{:S(2)}) collective-permute-start(f32[8,32,128]{2,1,0:T(8,128)S(1)} %get-tuple-element.25), channel_id=1, source_target_pairs={{0,16},{1,5},{2,18},{3,7},{4,20},{5,1},{6,22},{7,3},{8,24},{9,13},... | collective-permute-start | bytes 393224 | tf_op jit(solution)/shard_map/ppermute | solution.py:210
  33.8 0.7 %collective-permute-start.5 = (f32[8,32,128]{2,1,0:T(8,128)S(1)}, f32[8,32,128]{2,1,0:T(8,128)S(1)}, u32[]{:S(2)}, u32[]{:S(2)}) collective-permute-start(f32[8,32,128]{2,1,0:T(8,128)S(1)} %get-tuple-element.26), channel_id=1, source_target_pairs={{0,24},{1,7},{2,26},{3,5},{4,28},{5,3},{6,30},{7,1},{8,16},{9,15},... | collective-permute-start | bytes 393224 | tf_op jit(solution)/shard_map/ppermute | solution.py:210
  34.5 0.3 collective-permute-start.6
  34.8 1.9 %collective-permute-done.4 = f32[8,32,128]{2,1,0:T(8,128)S(1)} collective-permute-done((f32[8,32,128]{2,1,0:T(8,128)S(1)}, f32[8,32,128]{2,1,0:T(8,128)S(1)}, u32[]{:S(2)}, u32[]{:S(2)}) %collective-permute-start.4) | collective-permute-done | bytes 131104 | tf_op jit(solution)/shard_map/ppermute | solution.py:210
  36.7 3.2 %collective-permute-done.5 = f32[8,32,128]{2,1,0:T(8,128)S(1)} collective-permute-done((f32[8,32,128]{2,1,0:T(8,128)S(1)}, f32[8,32,128]{2,1,0:T(8,128)S(1)}, u32[]{:S(2)}, u32[]{:S(2)}) %collective-permute-start.5) | collective-permute-done | bytes 131104 | tf_op jit(solution)/shard_map/ppermute | solution.py:210
  39.9 0.0 collective-permute-done.6
  40.0 3.3 %collective-permute-start.7 = (f32[5,32,128]{2,1,0:T(8,128)S(1)}, f32[5,32,128]{2,1,0:T(8,128)S(1)}, u32[]{:S(2)}, u32[]{:S(2)}) collective-permute-start(f32[5,32,128]{2,1,0:T(8,128)S(1)} %get-tuple-element.19), channel_id=1, source_target_pairs={{0,64},{1,65},{2,66},{3,67},{4,68},{5,69},{6,70},{7,71},{8,72},{9,... | collective-permute-start | bytes 245768 | tf_op jit(solution)/shard_map/ppermute | solution.py:210
  43.3 1.1 %collective-permute-start.8 = (f32[5,32,128]{2,1,0:T(8,128)S(1)}, f32[5,32,128]{2,1,0:T(8,128)S(1)}, u32[]{:S(2)}, u32[]{:S(2)}) collective-permute-start(f32[5,32,128]{2,1,0:T(8,128)S(1)} %get-tuple-element.20), channel_id=1, source_target_pairs={{0,96},{1,97},{2,98},{3,99},{4,100},{5,101},{6,102},{7,103},{8,104... | collective-permute-start | bytes 245768 | tf_op jit(solution)/shard_map/ppermute | solution.py:210
  44.3 0.0 collective-permute-start.9
  44.4 1.8 %collective-permute-done.7 = f32[5,32,128]{2,1,0:T(8,128)S(1)} collective-permute-done((f32[5,32,128]{2,1,0:T(8,128)S(1)}, f32[5,32,128]{2,1,0:T(8,128)S(1)}, u32[]{:S(2)}, u32[]{:S(2)}) %collective-permute-start.7) | collective-permute-done | bytes 81952 | tf_op jit(solution)/shard_map/ppermute | solution.py:210
  46.2 2.8 %collective-permute-done.8 = f32[5,32,128]{2,1,0:T(8,128)S(1)} collective-permute-done((f32[5,32,128]{2,1,0:T(8,128)S(1)}, f32[5,32,128]{2,1,0:T(8,128)S(1)}, u32[]{:S(2)}, u32[]{:S(2)}) %collective-permute-start.8) | collective-permute-done | bytes 81952 | tf_op jit(solution)/shard_map/ppermute | solution.py:210
  48.9 0.0 collective-permute-done.9
  49.0 4.2 %factor.1.inverse_ref = f32[128,128]{1,0:T(8,128)S(1)} custom-call(f32[128,128]{1,0:T(8,128)S(1)} %bitcast.13), custom_call_target="tpu_custom_call" | custom-call | flops 49999998976 | bytes 131072 | tf_op jit(solution)/shard_map/factor/pallas_call | solution.py:169
  53.2 0.8 %project.1 = f32[32,128]{1,0:T(8,128)} custom-call(f32[128,128]{1,0:T(8,128)S(1)} %factor.1.inverse_ref, f32[1,32,128]{2,1,0:T(8,128)S(1)} %fusion.5.pieces_ref), custom_call_target="tpu_custom_call" | custom-call | tf_op jit(solution)/shard_map/project/pallas_call | solution.py:189
  (8 shorter events, 0.2 us)
Async XLA Ops:
  14.0 2.8 %collective-permute-start = (f32[68,32,128]{2,1,0:T(8,128)S(1)}, f32[68,32,128]{2,1,0:T(8,128)S(1)}, u32[]{:S(2)}, u32[]{:S(2)}) collective-permute-start(f32[68,32,128]{2,1,0:T(8,128)S(1)} %pad_maximum_fusion), channel_id=1, source_target_pairs={{0,1},{1,0},{2,3},{3,2},{4,5},{5,4},{6,7},{7,6},{8,9},{9,8},{10,11... | collective-permute-start | bytes 3342344 | tf_op jit(solution)/shard_map/ppermute | solution.py:200
  17.2 8.7 %collective-permute-start.1 = (f32[20,32,128]{2,1,0:T(8,128)S(1)}, f32[20,32,128]{2,1,0:T(8,128)S(1)}, u32[]{:S(2)}, u32[]{:S(2)}) collective-permute-start(f32[20,32,128]{2,1,0:T(8,128)S(1)} %get-tuple-element.28), channel_id=1, source_target_pairs={{0,4},{1,17},{2,6},{3,19},{4,0},{5,21},{6,2},{7,23},{8,12},{9,25},... | collective-permute-start | bytes 983048 | tf_op jit(solution)/shard_map/ppermute | solution.py:210
  20.4 9.0 %collective-permute-start.2 = (f32[20,32,128]{2,1,0:T(8,128)S(1)}, f32[20,32,128]{2,1,0:T(8,128)S(1)}, u32[]{:S(2)}, u32[]{:S(2)}) collective-permute-start(f32[20,32,128]{2,1,0:T(8,128)S(1)} %get-tuple-element.29), channel_id=1, source_target_pairs={{0,6},{1,25},{2,4},{3,27},{4,2},{5,29},{6,0},{7,31},{8,14},{9,17},... | collective-permute-start | bytes 983048 | tf_op jit(solution)/shard_map/ppermute | solution.py:210
  21.6 8.0 %collective-permute-start.3 = (f32[20,32,128]{2,1,0:T(8,128)S(1)}, f32[20,32,128]{2,1,0:T(8,128)S(1)}, u32[]{:S(2)}, u32[]{:S(2)}) collective-permute-start(f32[20,32,128]{2,1,0:T(8,128)S(1)} %get-tuple-element.30), channel_id=1, source_target_pairs={{0,2},{1,9},{2,0},{3,11},{4,6},{5,13},{6,4},{7,15},{8,10},{9,1},{1... | collective-permute-start | bytes 983048 | tf_op jit(solution)/shard_map/ppermute | solution.py:210
  29.8 6.9 %collective-permute-start.4 = (f32[8,32,128]{2,1,0:T(8,128)S(1)}, f32[8,32,128]{2,1,0:T(8,128)S(1)}, u32[]{:S(2)}, u32[]{:S(2)}) collective-permute-start(f32[8,32,128]{2,1,0:T(8,128)S(1)} %get-tuple-element.25), channel_id=1, source_target_pairs={{0,16},{1,5},{2,18},{3,7},{4,20},{5,1},{6,22},{7,3},{8,24},{9,13},... | collective-permute-start | bytes 393224 | tf_op jit(solution)/shard_map/ppermute | solution.py:210
  33.8 6.2 %collective-permute-start.5 = (f32[8,32,128]{2,1,0:T(8,128)S(1)}, f32[8,32,128]{2,1,0:T(8,128)S(1)}, u32[]{:S(2)}, u32[]{:S(2)}) collective-permute-start(f32[8,32,128]{2,1,0:T(8,128)S(1)} %get-tuple-element.26), channel_id=1, source_target_pairs={{0,24},{1,7},{2,26},{3,5},{4,28},{5,3},{6,30},{7,1},{8,16},{9,15},... | collective-permute-start | bytes 393224 | tf_op jit(solution)/shard_map/ppermute | solution.py:210
  34.5 5.5 %collective-permute-start.6 = (f32[8,32,128]{2,1,0:T(8,128)S(1)}, f32[8,32,128]{2,1,0:T(8,128)S(1)}, u32[]{:S(2)}, u32[]{:S(2)}) collective-permute-start(f32[8,32,128]{2,1,0:T(8,128)S(1)} %get-tuple-element.27), channel_id=1, source_target_pairs={{0,8},{1,3},{2,10},{3,1},{4,12},{5,7},{6,14},{7,5},{8,0},{9,11},{1... | collective-permute-start | bytes 393224 | tf_op jit(solution)/shard_map/ppermute | solution.py:210
  40.0 6.1 %collective-permute-start.7 = (f32[5,32,128]{2,1,0:T(8,128)S(1)}, f32[5,32,128]{2,1,0:T(8,128)S(1)}, u32[]{:S(2)}, u32[]{:S(2)}) collective-permute-start(f32[5,32,128]{2,1,0:T(8,128)S(1)} %get-tuple-element.19), channel_id=1, source_target_pairs={{0,64},{1,65},{2,66},{3,67},{4,68},{5,69},{6,70},{7,71},{8,72},{9,... | collective-permute-start | bytes 245768 | tf_op jit(solution)/shard_map/ppermute | solution.py:210
  43.3 5.7 %collective-permute-start.8 = (f32[5,32,128]{2,1,0:T(8,128)S(1)}, f32[5,32,128]{2,1,0:T(8,128)S(1)}, u32[]{:S(2)}, u32[]{:S(2)}) collective-permute-start(f32[5,32,128]{2,1,0:T(8,128)S(1)} %get-tuple-element.20), channel_id=1, source_target_pairs={{0,96},{1,97},{2,98},{3,99},{4,100},{5,101},{6,102},{7,103},{8,104... | collective-permute-start | bytes 245768 | tf_op jit(solution)/shard_map/ppermute | solution.py:210
  44.3 4.6 %collective-permute-start.9 = (f32[5,32,128]{2,1,0:T(8,128)S(1)}, f32[5,32,128]{2,1,0:T(8,128)S(1)}, u32[]{:S(2)}, u32[]{:S(2)}) collective-permute-start(f32[5,32,128]{2,1,0:T(8,128)S(1)} %get-tuple-element.21), channel_id=1, source_target_pairs={{0,32},{1,33},{2,34},{3,35},{4,36},{5,37},{6,38},{7,39},{8,40},{9,... | collective-permute-start | bytes 245768 | tf_op jit(solution)/shard_map/ppermute | solution.py:210

commit v4 on v3

--- a/solution.py
+++ b/solution.py
@@ -8,7 +8,7 @@
 SIDE = 4
 K = 128
 CHUNK = 256
-AHEAD = 3
+AHEAD = 4
 COLS = 512
 NT = (((1,), (1,)), ((), ()))
 
@@ -24,6 +24,24 @@
 
 def device(y, z, x, core):
     return ((y * SIDE + z) * SIDE + x) * 2 + core
+
+
+def lanes(rows):
+    return lax.broadcasted_iota(jnp.int32, (rows, K), 1)
+
+
+def pack(gram):
+    third = jnp.where(lanes(32) < 96, gram[64:96], pltpu.roll(gram[:32], 96, 1))
+    second = jnp.where(lanes(16) < 64, gram[32:48], pltpu.roll(gram[48:64], 64, 1))
+    return jnp.concatenate([gram[96:], third, second], axis=0)
+
+
+def unpack(packed):
+    third, second = packed[32:64], packed[64:80]
+    low = [pltpu.roll(third, 32, 1), second, pltpu.roll(second, 64, 1), third, packed[:32]]
+    low = jnp.concatenate(low, axis=0)
+    row = lax.broadcasted_iota(jnp.int32, (K, K), 0)
+    return jnp.where(row // 32 >= lanes(K) // 32, low, low.T)
 
 
 def sketch_kernel(place_ref, slab_ref, omega_ref, gram_ref, mine_ref, other_ref, slab_v, omega_v, beside, above, sems, omega_sem):
@@ -44,16 +62,24 @@
     omega_copy.wait()
     for i in range(1, AHEAD):
         copy(i).start()
+    def keep(i, sketch):
+        at = pl.ds(i * CHUNK, CHUNK)
+        beside[at, :K], beside[at, K:] = split(sketch)
+        above[:K, at], above[K:, at] = split(sketch.T)
+
+    last = None
     for i in range(chunks):
         copy(i).wait()
         if i + AHEAD < chunks:
             copy(i + AHEAD).start()
-        at = pl.ds(i * CHUNK, CHUNK)
-        sketch = jnp.dot(slab_v[at, :], omega_v[...], preferred_element_type=jnp.float32)
-        beside[at, :K], beside[at, K:] = split(sketch)
-        above[:K, at], above[K:, at] = split(sketch.T)
+        block = slab_v[pl.ds(i * CHUNK, CHUNK), :]
+        sketch = jnp.dot(block, omega_v[...], preferred_element_type=jnp.float32)
+        if i > 0:
+            keep(i - 1, last)
+        last = sketch
+    keep(chunks - 1, last)
     gram = jnp.dot(above[...], beside[...], preferred_element_type=jnp.float32)
-    gram_ref[...] = (gram[K:, K:] + (gram[:K, K:] + gram[K:, :K])) + gram[:K, :K]
+    gram_ref[...] = pack((gram[K:, K:] + (gram[:K, K:] + gram[K:, :K])) + gram[:K, :K])
 
     y, z, x, core = (place_ref[i] for i in range(4))
     first = core == 0
@@ -64,8 +90,10 @@
             to_y, to_z, to_x = place_of(n * (COLS // 64) + chip)
             even, odd = tile[chip, 0], tile[chip, 1]
             by_y, by_z, by_x = turn(to_y, y), turn(to_z, z), turn(to_x, x)
-            mine_at = jnp.where(first, by_x, by_z), SIDE * jnp.where(first, by_z, by_x) + by_y
-            other_at = jnp.where(first, by_z, by_x), SIDE * jnp.where(first, by_x, by_z) + by_y
+            even_at = by_x, SIDE * by_z + by_y
+            odd_at = by_z, SIDE * by_x + by_y
+            mine_at = [jnp.where(first, p, q) for p, q in zip(even_at, odd_at)]
+            other_at = [jnp.where(first, q, p) for p, q in zip(even_at, odd_at)]
             mine_ref[mine_at[0], mine_at[1]] = jnp.where(first, even, odd)
             other_ref[other_at[0], other_at[1]] = jnp.where(first, odd, even)
 
@@ -77,7 +105,7 @@
     half = jax.ShapeDtypeStruct((SIDE, SIDE * SIDE, 32, K), jnp.float32)
     return pl.pallas_call(
         sketch_kernel,
-        out_shape=(jax.ShapeDtypeStruct((K, K), jnp.float32), half, half),
+        out_shape=(jax.ShapeDtypeStruct((80, K), jnp.float32), half, half),
         in_specs=[pl.BlockSpec(memory_space=pltpu.SMEM), hbm, hbm],
         out_specs=(vmem,) * 3,
         scratch_shapes=[
@@ -94,6 +122,10 @@
         ),
         name="sketch",
     )(place, slab, omega)
+
+
+AXES = (2, 1), (1, 2), (0, 0)
+MASKS = 3, 1, 2
 
 
 def factor_rows(blocks):
@@ -158,42 +190,30 @@
     return done
 
 
-def factor_kernel(gram_ref, inverse_ref):
-    blocks = [gram_ref[pl.ds(8 * b, 8), :] for b in range(K // 8)]
-    for b, rows in enumerate(factor_rows(blocks)):
-        inverse_ref[pl.ds(8 * b, 8), :] = rows
-
-
-def factor_call(gram):
+def finish_kernel(part_ref, gram_ref, near_ref, other_ref, across_ref, out_ref, inverse):
+    columns = part_ref.shape[0]
+    own = jnp.concatenate([part_ref[...], gram_ref[...]], axis=0)
+    total = (own + across_ref[...]) + (near_ref[...] + other_ref[...])
+    gram = unpack(total[columns:])
+    for b, rows in enumerate(factor_rows([gram[8 * b : 8 * b + 8] for b in range(K // 8)])):
+        inverse[pl.ds(8 * b, 8), :] = rows
+    out_ref[...] = lax.dot_general(
+        total[:columns], inverse[...], NT, precision=lax.Precision.HIGHEST, preferred_element_type=jnp.float32
+    )
+
+
+def finish_call(part, gram, got):
     vmem = pl.BlockSpec(memory_space=pltpu.VMEM)
     return pl.pallas_call(
-        factor_kernel,
-        out_shape=jax.ShapeDtypeStruct((K, K), jnp.float32),
-        in_specs=[vmem],
+        finish_kernel,
+        out_shape=jax.ShapeDtypeStruct(part.shape, jnp.float32),
+        in_specs=[vmem] * 5,
         out_specs=vmem,
+        scratch_shapes=[pltpu.VMEM((K, K), jnp.float32)],
         compiler_params=pltpu.CompilerParams(vmem_limit_bytes=8 * 2**20),
-        cost_estimate=pl.CostEstimate(flops=5 * 10**10, bytes_accessed=2**17, transcendentals=0),
-        name="factor",
-    )(gram)
-
-
-def project_kernel(inverse_ref, pieces_ref, out_ref):
-    total = jnp.sum(pieces_ref[...], axis=0)
-    out_ref[...] = lax.dot_general(
-        total, inverse_ref[...], NT, precision=lax.Precision.HIGHEST, preferred_element_type=jnp.float32
-    )
-
-
-def project_call(inverse, pieces):
-    vmem = pl.BlockSpec(memory_space=pltpu.VMEM)
-    return pl.pallas_call(
-        project_kernel,
-        out_shape=jax.ShapeDtypeStruct((pieces.shape[1], K), jnp.float32),
-        in_specs=[vmem, vmem],
-        out_specs=vmem,
-        compiler_params=pltpu.CompilerParams(vmem_limit_bytes=8 * 2**20),
-        name="project",
-    )(inverse, pieces)
+        cost_estimate=pl.CostEstimate(flops=10**9, bytes_accessed=2**20, transcendentals=0),
+        name="finish",
+    )(part, gram, *got)
 
 
 def swap_cores(array):
@@ -203,9 +223,9 @@
 def swap_chips(array, axes, mask):
     pairs = []
     for chip in range(SIDE**3):
-        for core in range(2):
+        for core, axis in enumerate(axes):
             target = list(place_of(chip))
-            target[axes[core]] ^= mask
+            target[axis] ^= mask
             pairs.append((2 * chip + core, device(*target, core)))
     return lax.ppermute(array, "rows", pairs)
 
@@ -217,20 +237,18 @@
     test_matrix = pltpu.with_memory_space_constraint(test_matrix, pltpu.HBM)
     gram, mine, other = sketch_call(place, slab, test_matrix)
 
-    pieces = SIDE**3
-    mine, other = mine.reshape(pieces, 32, K), other.reshape(pieces, 32, K)
-    gram = gram.reshape(-1, 32, K)
+    rows = SIDE**3 * 32
+    mine, other = mine.reshape(rows, K), other.reshape(rows, K)
     got = swap_cores(jnp.concatenate([other, gram]))
-    part, gram = mine + got[:pieces], gram + got[pieces:]
-    for axes in ((2, 1), (1, 2), (0, 0)):
-        pieces //= 4
-        quarters = [part[i * pieces : (i + 1) * pieces] for i in range(4)]
-        got = [
-            swap_chips(jnp.concatenate([quarters[i], gram]), axes, mask) for i, mask in ((3, 2), (1, 3), (2, 1))
-        ]
-        part = (quarters[0] + got[0][:pieces]) + (got[1][:pieces] + got[2][:pieces])
-        gram = (gram + got[0][pieces:]) + (got[1][pieces:] + got[2][pieces:])
-    return project_call(factor_call(gram.reshape(K, K)), part).T
+    part, gram = mine + got[:rows], gram + got[rows:]
+    for number, axes in enumerate(AXES):
+        rows //= 4
+        stay, *leave = (part[i * rows : (i + 1) * rows] for i in range(4))
+        got = [swap_chips(jnp.concatenate([piece, gram]), axes, mask) for piece, mask in zip(leave, MASKS)]
+        if number + 1 == len(AXES):
+            return finish_call(stay, gram, got).T
+        part = (stay + got[2][:rows]) + (got[0][:rows] + got[1][:rows])
+        gram = (gram + got[2][rows:]) + (got[0][rows:] + got[1][rows:])
 
 
 def solution(mesh):

time: 54.1 us -> 53.4 us (0.987)
    pallas_call x3 -> x2, Pallas kernels: 18.8 us -> 18.7 us  [the longest x1 13.5 us: sketch_call(): pl.pallas_call(sketch_kernel, out_shape=(jax.ShapeDtypeStruct((80, K), jn...]
  transfers between devices with their start and end apart: 10 -> 10, of which waited for: 8 -> 9; matrix products, arithmetic and copies ran while one was open for 0% -> 0% of each run, Pallas kernels for 0% -> 0%
where the time goes in v4:
time: 53.4 us; the launch traced here: 53.3 us
  waiting for transfers between devices  20.1 us (38%)
  Pallas kernels  18.7 us (35%)
  starting transfers between devices  13.7 us (26%)
    ppermute x9, waiting for transfers between devices, swap_chips(): return lax.ppermute(array, 'rows', pairs)  17.4 us
    ppermute x9, starting transfers between devices, swap_chips(): return lax.ppermute(array, 'rows', pairs)  13.6 us
    pallas_call x1, Pallas kernels, sketch_call(): pl.pallas_call(sketch_kernel, out_shape=(jax.ShapeDtypeStruct((80, K), jn...  13.5 us
    pallas_call x1, Pallas kernels, finish_call(): pl.pallas_call(finish_kernel, out_shape=jax.ShapeDtypeStruct(part.shape,...  5.28 us
    ppermute x1, waiting for transfers between devices, swap_cores(): lax.ppermute(array, 'rows', [(i, i ^ 1) for i in range(2 * SIDE ** 3)])  2.71 us
  transfers between devices with their start and end apart: 10, of which 9 were waited for; matrix products, arithmetic and copies ran while one was open for 0% of the time, Pallas kernels for 0%

profile of v4, /device:TPU:0, one launch (start us, length us, event | category | flops | bytes accessed | tf_op | source)
XLA Modules:
  0.0 53.3 jit_solution(3042542216903437462)
XLA Ops:
  0.0 0.1 pad_add_fusion.place_ref
  0.1 13.5 %sketch.1 = (f32[80,128]{1,0:T(8,128)S(1)}, f32[4,16,32,128]{3,2,1,0:T(8,128)S(1)}, f32[4,16,32,128]{3,2,1,0:T(8,128)S(1)}) custom-call(s32[4]{0:T(128)S(1)} %pad_add_fusion.place_ref, bf16[2048,4096]{1,0:T(8,128)(2,1)} %slab_ref.1, bf16[4096,128]{1,0:T(8,128)(2,1)} %omega_ref.1), custom_call_target="tpu_custom_call" | custom-call | flops 6442450944 | bytes 16777216 | tf_op jit(solution)/shard_map/sketch/pallas_call | solution.py:106
  13.5 0.1 pad_maximum_fusion
  13.6 0.1 collective-permute-start
  13.7 2.7 %collective-permute-done = f32[2128,128]{1,0:T(8,128)S(1)} collective-permute-done((f32[2128,128]{1,0:T(8,128)S(1)}, f32[2128,128]{1,0:T(8,128)S(1)}, u32[]{:S(2)}, u32[]{:S(2)}) %collective-permute-start) | collective-permute-done | bytes 1089568 | tf_op jit(solution)/shard_map/ppermute | solution.py:220
  16.4 0.1 slice_add_fusion
  16.6 0.1 fusion.4
  16.6 0.1 pad_maximum_fusion.3
  16.7 3.2 %collective-permute-start.1 = (f32[592,128]{1,0:T(8,128)S(1)}, f32[592,128]{1,0:T(8,128)S(1)}, u32[]{:S(2)}, u32[]{:S(2)}) collective-permute-start(f32[592,128]{1,0:T(8,128)S(1)} %get-tuple-element.27), channel_id=1, source_target_pairs={{0,4},{1,17},{2,6},{3,19},{4,0},{5,21},{6,2},{7,23},{8,12},{9,25},... | collective-permute-start | bytes 909320 | tf_op jit(solution)/shard_map/ppermute | solution.py:230
  19.9 1.1 %collective-permute-start.2 = (f32[592,128]{1,0:T(8,128)S(1)}, f32[592,128]{1,0:T(8,128)S(1)}, u32[]{:S(2)}, u32[]{:S(2)}) collective-permute-start(f32[592,128]{1,0:T(8,128)S(1)} %get-tuple-element.28), channel_id=1, source_target_pairs={{0,6},{1,25},{2,4},{3,27},{4,2},{5,29},{6,0},{7,31},{8,14},{9,17},... | collective-permute-start | bytes 909320 | tf_op jit(solution)/shard_map/ppermute | solution.py:230
  21.0 0.0 collective-permute-start.3
  21.0 4.1 %collective-permute-done.1 = f32[592,128]{1,0:T(8,128)S(1)} collective-permute-done((f32[592,128]{1,0:T(8,128)S(1)}, f32[592,128]{1,0:T(8,128)S(1)}, u32[]{:S(2)}, u32[]{:S(2)}) %collective-permute-start.1) | collective-permute-done | bytes 303136 | tf_op jit(solution)/shard_map/ppermute | solution.py:230
  25.1 3.2 %collective-permute-done.2 = f32[592,128]{1,0:T(8,128)S(1)} collective-permute-done((f32[592,128]{1,0:T(8,128)S(1)}, f32[592,128]{1,0:T(8,128)S(1)}, u32[]{:S(2)}, u32[]{:S(2)}) %collective-permute-start.2) | collective-permute-done | bytes 303136 | tf_op jit(solution)/shard_map/ppermute | solution.py:230
  28.3 0.2 collective-permute-done.3
  28.6 0.1 fusion
  28.7 4.0 %collective-permute-start.4 = (f32[208,128]{1,0:T(8,128)S(1)}, f32[208,128]{1,0:T(8,128)S(1)}, u32[]{:S(2)}, u32[]{:S(2)}) collective-permute-start(f32[208,128]{1,0:T(8,128)S(1)} %get-tuple-element.24), channel_id=1, source_target_pairs={{0,16},{1,5},{2,18},{3,7},{4,20},{5,1},{6,22},{7,3},{8,24},{9,13},... | collective-permute-start | bytes 319496 | tf_op jit(solution)/shard_map/ppermute | solution.py:230
  32.7 0.7 %collective-permute-start.5 = (f32[208,128]{1,0:T(8,128)S(1)}, f32[208,128]{1,0:T(8,128)S(1)}, u32[]{:S(2)}, u32[]{:S(2)}) collective-permute-start(f32[208,128]{1,0:T(8,128)S(1)} %get-tuple-element.25), channel_id=1, source_target_pairs={{0,24},{1,7},{2,26},{3,5},{4,28},{5,3},{6,30},{7,1},{8,16},{9,15},... | collective-permute-start | bytes 319496 | tf_op jit(solution)/shard_map/ppermute | solution.py:230
  33.4 0.3 collective-permute-start.6
  33.7 1.7 %collective-permute-done.4 = f32[208,128]{1,0:T(8,128)S(1)} collective-permute-done((f32[208,128]{1,0:T(8,128)S(1)}, f32[208,128]{1,0:T(8,128)S(1)}, u32[]{:S(2)}, u32[]{:S(2)}) %collective-permute-start.4) | collective-permute-done | bytes 106528 | tf_op jit(solution)/shard_map/ppermute | solution.py:230
  35.4 3.2 %collective-permute-done.5 = f32[208,128]{1,0:T(8,128)S(1)} collective-permute-done((f32[208,128]{1,0:T(8,128)S(1)}, f32[208,128]{1,0:T(8,128)S(1)}, u32[]{:S(2)}, u32[]{:S(2)}) %collective-permute-start.5) | collective-permute-done | bytes 106528 | tf_op jit(solution)/shard_map/ppermute | solution.py:230
  38.6 0.0 collective-permute-done.6
  38.7 3.3 %collective-permute-start.9 = (f32[112,128]{1,0:T(8,128)S(1)}, f32[112,128]{1,0:T(8,128)S(1)}, u32[]{:S(2)}, u32[]{:S(2)}) collective-permute-start(f32[112,128]{1,0:T(8,128)S(1)} %get-tuple-element.21), channel_id=1, source_target_pairs={{0,64},{1,65},{2,66},{3,67},{4,68},{5,69},{6,70},{7,71},{8,72},{9,... | collective-permute-start | bytes 172040 | tf_op jit(solution)/shard_map/ppermute | solution.py:230
  41.9 0.7 %collective-permute-start.8 = (f32[112,128]{1,0:T(8,128)S(1)}, f32[112,128]{1,0:T(8,128)S(1)}, u32[]{:S(2)}, u32[]{:S(2)}) collective-permute-start(f32[112,128]{1,0:T(8,128)S(1)} %get-tuple-element.22), channel_id=1, source_target_pairs={{0,32},{1,33},{2,34},{3,35},{4,36},{5,37},{6,38},{7,39},{8,40},{9,... | collective-permute-start | bytes 172040 | tf_op jit(solution)/shard_map/ppermute | solution.py:230
  42.6 0.4 collective-permute-start.7
  43.0 1.5 %collective-permute-done.9.across_ref = f32[112,128]{1,0:T(8,128)S(1)} collective-permute-done((f32[112,128]{1,0:T(8,128)S(1)}, f32[112,128]{1,0:T(8,128)S(1)}, u32[]{:S(2)}, u32[]{:S(2)}) %collective-permute-start.9) | collective-permute-done | bytes 57376 | tf_op jit(solution)/shard_map/ppermute | solution.py:230
  44.5 1.6 %collective-permute-done.8.other_ref = f32[112,128]{1,0:T(8,128)S(1)} collective-permute-done((f32[112,128]{1,0:T(8,128)S(1)}, f32[112,128]{1,0:T(8,128)S(1)}, u32[]{:S(2)}, u32[]{:S(2)}) %collective-permute-start.8) | collective-permute-done | bytes 57376 | tf_op jit(solution)/shard_map/ppermute | solution.py:230
  46.1 1.9 %collective-permute-done.7.near_ref = f32[112,128]{1,0:T(8,128)S(1)} collective-permute-done((f32[112,128]{1,0:T(8,128)S(1)}, f32[112,128]{1,0:T(8,128)S(1)}, u32[]{:S(2)}, u32[]{:S(2)}) %collective-permute-start.7) | collective-permute-done | bytes 57376 | tf_op jit(solution)/shard_map/ppermute | solution.py:230
  48.0 5.3 %finish.1 = f32[32,128]{1,0:T(8,128)} custom-call(f32[32,128]{1,0:T(8,128)S(1)} %get-tuple-element.20.part_ref, f32[80,128]{1,0:T(8,128)S(1)} %fusion.2.gram_ref, f32[112,128]{1,0:T(8,128)S(1)} %collective-permute-done.7.near_ref, f32[112,128]{1,0:T(8,128)S(1)} %collective-permute-done.8.other_ref, f32[112,128]{1,0:T(8,128)S(1)} %collective-permute-done.9.across_ref), custom_call_target="tpu_custom_call" | custom-call | flops 1000000000 | bytes 1048576 | tf_op jit(solution)/shard_map/finish/pallas_call | solution.py:207
  (8 shorter events, 0.1 us)
Async XLA Ops:
  13.6 2.8 %collective-permute-start = (f32[2128,128]{1,0:T(8,128)S(1)}, f32[2128,128]{1,0:T(8,128)S(1)}, u32[]{:S(2)}, u32[]{:S(2)}) collective-permute-start(f32[2128,128]{1,0:T(8,128)S(1)} %pad_maximum_fusion), channel_id=1, source_target_pairs={{0,1},{1,0},{2,3},{3,2},{4,5},{5,4},{6,7},{7,6},{8,9},{9,8},{10,11... | collective-permute-start | bytes 3268616 | tf_op jit(solution)/shard_map/ppermute | solution.py:220
  16.7 8.4 %collective-permute-start.1 = (f32[592,128]{1,0:T(8,128)S(1)}, f32[592,128]{1,0:T(8,128)S(1)}, u32[]{:S(2)}, u32[]{:S(2)}) collective-permute-start(f32[592,128]{1,0:T(8,128)S(1)} %get-tuple-element.27), channel_id=1, source_target_pairs={{0,4},{1,17},{2,6},{3,19},{4,0},{5,21},{6,2},{7,23},{8,12},{9,25},... | collective-permute-start | bytes 909320 | tf_op jit(solution)/shard_map/ppermute | solution.py:230
  19.9 8.4 %collective-permute-start.2 = (f32[592,128]{1,0:T(8,128)S(1)}, f32[592,128]{1,0:T(8,128)S(1)}, u32[]{:S(2)}, u32[]{:S(2)}) collective-permute-start(f32[592,128]{1,0:T(8,128)S(1)} %get-tuple-element.28), channel_id=1, source_target_pairs={{0,6},{1,25},{2,4},{3,27},{4,2},{5,29},{6,0},{7,31},{8,14},{9,17},... | collective-permute-start | bytes 909320 | tf_op jit(solution)/shard_map/ppermute | solution.py:230
  21.0 7.5 %collective-permute-start.3 = (f32[592,128]{1,0:T(8,128)S(1)}, f32[592,128]{1,0:T(8,128)S(1)}, u32[]{:S(2)}, u32[]{:S(2)}) collective-permute-start(f32[592,128]{1,0:T(8,128)S(1)} %get-tuple-element.29), channel_id=1, source_target_pairs={{0,2},{1,9},{2,0},{3,11},{4,6},{5,13},{6,4},{7,15},{8,10},{9,1},{1... | collective-permute-start | bytes 909320 | tf_op jit(solution)/shard_map/ppermute | solution.py:230
  28.7 6.6 %collective-permute-start.4 = (f32[208,128]{1,0:T(8,128)S(1)}, f32[208,128]{1,0:T(8,128)S(1)}, u32[]{:S(2)}, u32[]{:S(2)}) collective-permute-start(f32[208,128]{1,0:T(8,128)S(1)} %get-tuple-element.24), channel_id=1, source_target_pairs={{0,16},{1,5},{2,18},{3,7},{4,20},{5,1},{6,22},{7,3},{8,24},{9,13},... | collective-permute-start | bytes 319496 | tf_op jit(solution)/shard_map/ppermute | solution.py:230
  32.7 5.9 %collective-permute-start.5 = (f32[208,128]{1,0:T(8,128)S(1)}, f32[208,128]{1,0:T(8,128)S(1)}, u32[]{:S(2)}, u32[]{:S(2)}) collective-permute-start(f32[208,128]{1,0:T(8,128)S(1)} %get-tuple-element.25), channel_id=1, source_target_pairs={{0,24},{1,7},{2,26},{3,5},{4,28},{5,3},{6,30},{7,1},{8,16},{9,15},... | collective-permute-start | bytes 319496 | tf_op jit(solution)/shard_map/ppermute | solution.py:230
  33.4 5.2 %collective-permute-start.6 = (f32[208,128]{1,0:T(8,128)S(1)}, f32[208,128]{1,0:T(8,128)S(1)}, u32[]{:S(2)}, u32[]{:S(2)}) collective-permute-start(f32[208,128]{1,0:T(8,128)S(1)} %get-tuple-element.26), channel_id=1, source_target_pairs={{0,8},{1,3},{2,10},{3,1},{4,12},{5,7},{6,14},{7,5},{8,0},{9,11},{1... | collective-permute-start | bytes 319496 | tf_op jit(solution)/shard_map/ppermute | solution.py:230
  38.7 5.8 %collective-permute-start.9 = (f32[112,128]{1,0:T(8,128)S(1)}, f32[112,128]{1,0:T(8,128)S(1)}, u32[]{:S(2)}, u32[]{:S(2)}) collective-permute-start(f32[112,128]{1,0:T(8,128)S(1)} %get-tuple-element.21), channel_id=1, source_target_pairs={{0,64},{1,65},{2,66},{3,67},{4,68},{5,69},{6,70},{7,71},{8,72},{9,... | collective-permute-start | bytes 172040 | tf_op jit(solution)/shard_map/ppermute | solution.py:230
  41.9 4.2 %collective-permute-start.8 = (f32[112,128]{1,0:T(8,128)S(1)}, f32[112,128]{1,0:T(8,128)S(1)}, u32[]{:S(2)}, u32[]{:S(2)}) collective-permute-start(f32[112,128]{1,0:T(8,128)S(1)} %get-tuple-element.22), channel_id=1, source_target_pairs={{0,32},{1,33},{2,34},{3,35},{4,36},{5,37},{6,38},{7,39},{8,40},{9,... | collective-permute-start | bytes 172040 | tf_op jit(solution)/shard_map/ppermute | solution.py:230
  42.6 5.4 %collective-permute-start.7 = (f32[112,128]{1,0:T(8,128)S(1)}, f32[112,128]{1,0:T(8,128)S(1)}, u32[]{:S(2)}, u32[]{:S(2)}) collective-permute-start(f32[112,128]{1,0:T(8,128)S(1)} %get-tuple-element.23), channel_id=1, source_target_pairs={{0,96},{1,97},{2,98},{3,99},{4,100},{5,101},{6,102},{7,103},{8,104... | collective-permute-start | bytes 172040 | tf_op jit(solution)/shard_map/ppermute | solution.py:230

commit v5 on v4

--- a/solution.py
+++ b/solution.py
@@ -167,26 +167,16 @@
         done.append(jnp.where(lane <= first + sublane, result, 0.0))
         if b + 1 == count:
             break
-        target = blocks[b + 1]
-        factors = [column(target, first + k) for k in range(8)]
-        target = jnp.where(inside, 0.0, target)
-        for k in range(8):
-            factor = factors[k] * inverse[k]
-            for m in range(k + 1, 8):
-                factors[m] = factors[m] - factor * entry[m, k]
-            target = target - factor * rows[k]
-        blocks[b + 1] = target
-        solved = [None] * 8
-        for k in reversed(range(8)):
-            value = rows[k] * inverse[k]
-            for m in range(k + 1, 8):
-                value = value - lower[m, k] * solved[m]
-            solved[k] = value
-        for i in range(b + 2, count):
-            products = [column(blocks[i], first + k) * solved[k] for k in range(8)]
-            while len(products) > 1:
-                products = [products[p] + products[p + 1] for p in range(0, len(products), 2)]
-            blocks[i] = jnp.where(inside, 0.0, blocks[i]) - products[0]
+        for i in range(b + 1, count):
+            target = blocks[i]
+            factors = [column(target, first + k) for k in range(8)]
+            target = jnp.where(inside, 0.0, target)
+            for k in range(8):
+                factor = factors[k] * inverse[k]
+                for m in range(k + 1, 8):
+                    factors[m] = factors[m] - factor * entry[m, k]
+                target = target - factor * rows[k]
+            blocks[i] = target
     return done
 
 

time: 53.4 us -> 53.2 us (level)
  no operation moved by 1% of the time
where the time goes in v5:
time: 53.2 us; the launch traced here: 53.1 us
  waiting for transfers between devices  20.1 us (38%)
  Pallas kernels  18.6 us (35%)
  starting transfers between devices  13.7 us (26%)
    ppermute x9, waiting for transfers between devices, swap_chips(): return lax.ppermute(array, 'rows', pairs)  17.4 us
    ppermute x9, starting transfers between devices, swap_chips(): return lax.ppermute(array, 'rows', pairs)  13.6 us
    pallas_call x1, Pallas kernels, sketch_call(): pl.pallas_call(sketch_kernel, out_shape=(jax.ShapeDtypeStruct((80, K), jn...  13.5 us
    pallas_call x1, Pallas kernels, finish_call(): pl.pallas_call(finish_kernel, out_shape=jax.ShapeDtypeStruct(part.shape,...  5.12 us
    ppermute x1, waiting for transfers between devices, swap_cores(): lax.ppermute(array, 'rows', [(i, i ^ 1) for i in range(2 * SIDE ** 3)])  2.71 us
  transfers between devices with their start and end apart: 10, of which 9 were waited for; matrix products, arithmetic and copies ran while one was open for 0% of the time, Pallas kernels for 0%

profile of v5, /device:TPU:0, one launch (start us, length us, event | category | flops | bytes accessed | tf_op | source)
XLA Modules:
  0.0 53.1 jit_solution(10695443506373697054)
XLA Ops:
  0.0 0.1 pad_add_fusion.place_ref
  0.1 13.5 %sketch.1 = (f32[80,128]{1,0:T(8,128)S(1)}, f32[4,16,32,128]{3,2,1,0:T(8,128)S(1)}, f32[4,16,32,128]{3,2,1,0:T(8,128)S(1)}) custom-call(s32[4]{0:T(128)S(1)} %pad_add_fusion.place_ref, bf16[2048,4096]{1,0:T(8,128)(2,1)} %slab_ref.1, bf16[4096,128]{1,0:T(8,128)(2,1)} %omega_ref.1), custom_call_target="tpu_custom_call" | custom-call | flops 6442450944 | bytes 16777216 | tf_op jit(solution)/shard_map/sketch/pallas_call | solution.py:106
  13.5 0.1 pad_maximum_fusion
  13.6 0.1 collective-permute-start
  13.7 2.7 %collective-permute-done = f32[2128,128]{1,0:T(8,128)S(1)} collective-permute-done((f32[2128,128]{1,0:T(8,128)S(1)}, f32[2128,128]{1,0:T(8,128)S(1)}, u32[]{:S(2)}, u32[]{:S(2)}) %collective-permute-start) | collective-permute-done | bytes 1089568 | tf_op jit(solution)/shard_map/ppermute | solution.py:210
  16.4 0.1 slice_add_fusion
  16.6 0.1 fusion.4
  16.6 0.1 pad_maximum_fusion.3
  16.7 3.2 %collective-permute-start.1 = (f32[592,128]{1,0:T(8,128)S(1)}, f32[592,128]{1,0:T(8,128)S(1)}, u32[]{:S(2)}, u32[]{:S(2)}) collective-permute-start(f32[592,128]{1,0:T(8,128)S(1)} %get-tuple-element.27), channel_id=1, source_target_pairs={{0,4},{1,17},{2,6},{3,19},{4,0},{5,21},{6,2},{7,23},{8,12},{9,25},... | collective-permute-start | bytes 909320 | tf_op jit(solution)/shard_map/ppermute | solution.py:220
  19.9 1.1 %collective-permute-start.2 = (f32[592,128]{1,0:T(8,128)S(1)}, f32[592,128]{1,0:T(8,128)S(1)}, u32[]{:S(2)}, u32[]{:S(2)}) collective-permute-start(f32[592,128]{1,0:T(8,128)S(1)} %get-tuple-element.28), channel_id=1, source_target_pairs={{0,6},{1,25},{2,4},{3,27},{4,2},{5,29},{6,0},{7,31},{8,14},{9,17},... | collective-permute-start | bytes 909320 | tf_op jit(solution)/shard_map/ppermute | solution.py:220
  21.0 0.0 collective-permute-start.3
  21.0 4.1 %collective-permute-done.1 = f32[592,128]{1,0:T(8,128)S(1)} collective-permute-done((f32[592,128]{1,0:T(8,128)S(1)}, f32[592,128]{1,0:T(8,128)S(1)}, u32[]{:S(2)}, u32[]{:S(2)}) %collective-permute-start.1) | collective-permute-done | bytes 303136 | tf_op jit(solution)/shard_map/ppermute | solution.py:220
  25.1 3.2 %collective-permute-done.2 = f32[592,128]{1,0:T(8,128)S(1)} collective-permute-done((f32[592,128]{1,0:T(8,128)S(1)}, f32[592,128]{1,0:T(8,128)S(1)}, u32[]{:S(2)}, u32[]{:S(2)}) %collective-permute-start.2) | collective-permute-done | bytes 303136 | tf_op jit(solution)/shard_map/ppermute | solution.py:220
  28.3 0.2 collective-permute-done.3
  28.6 0.1 fusion
  28.7 4.0 %collective-permute-start.4 = (f32[208,128]{1,0:T(8,128)S(1)}, f32[208,128]{1,0:T(8,128)S(1)}, u32[]{:S(2)}, u32[]{:S(2)}) collective-permute-start(f32[208,128]{1,0:T(8,128)S(1)} %get-tuple-element.24), channel_id=1, source_target_pairs={{0,16},{1,5},{2,18},{3,7},{4,20},{5,1},{6,22},{7,3},{8,24},{9,13},... | collective-permute-start | bytes 319496 | tf_op jit(solution)/shard_map/ppermute | solution.py:220
  32.7 0.7 %collective-permute-start.5 = (f32[208,128]{1,0:T(8,128)S(1)}, f32[208,128]{1,0:T(8,128)S(1)}, u32[]{:S(2)}, u32[]{:S(2)}) collective-permute-start(f32[208,128]{1,0:T(8,128)S(1)} %get-tuple-element.25), channel_id=1, source_target_pairs={{0,24},{1,7},{2,26},{3,5},{4,28},{5,3},{6,30},{7,1},{8,16},{9,15},... | collective-permute-start | bytes 319496 | tf_op jit(solution)/shard_map/ppermute | solution.py:220
  33.4 0.3 collective-permute-start.6
  33.7 1.7 %collective-permute-done.4 = f32[208,128]{1,0:T(8,128)S(1)} collective-permute-done((f32[208,128]{1,0:T(8,128)S(1)}, f32[208,128]{1,0:T(8,128)S(1)}, u32[]{:S(2)}, u32[]{:S(2)}) %collective-permute-start.4) | collective-permute-done | bytes 106528 | tf_op jit(solution)/shard_map/ppermute | solution.py:220
  35.4 3.2 %collective-permute-done.5 = f32[208,128]{1,0:T(8,128)S(1)} collective-permute-done((f32[208,128]{1,0:T(8,128)S(1)}, f32[208,128]{1,0:T(8,128)S(1)}, u32[]{:S(2)}, u32[]{:S(2)}) %collective-permute-start.5) | collective-permute-done | bytes 106528 | tf_op jit(solution)/shard_map/ppermute | solution.py:220
  38.6 0.0 collective-permute-done.6
  38.7 3.3 %collective-permute-start.9 = (f32[112,128]{1,0:T(8,128)S(1)}, f32[112,128]{1,0:T(8,128)S(1)}, u32[]{:S(2)}, u32[]{:S(2)}) collective-permute-start(f32[112,128]{1,0:T(8,128)S(1)} %get-tuple-element.21), channel_id=1, source_target_pairs={{0,64},{1,65},{2,66},{3,67},{4,68},{5,69},{6,70},{7,71},{8,72},{9,... | collective-permute-start | bytes 172040 | tf_op jit(solution)/shard_map/ppermute | solution.py:220
  41.9 0.7 %collective-permute-start.8 = (f32[112,128]{1,0:T(8,128)S(1)}, f32[112,128]{1,0:T(8,128)S(1)}, u32[]{:S(2)}, u32[]{:S(2)}) collective-permute-start(f32[112,128]{1,0:T(8,128)S(1)} %get-tuple-element.22), channel_id=1, source_target_pairs={{0,32},{1,33},{2,34},{3,35},{4,36},{5,37},{6,38},{7,39},{8,40},{9,... | collective-permute-start | bytes 172040 | tf_op jit(solution)/shard_map/ppermute | solution.py:220
  42.6 0.4 collective-permute-start.7
  43.0 1.5 %collective-permute-done.9.across_ref = f32[112,128]{1,0:T(8,128)S(1)} collective-permute-done((f32[112,128]{1,0:T(8,128)S(1)}, f32[112,128]{1,0:T(8,128)S(1)}, u32[]{:S(2)}, u32[]{:S(2)}) %collective-permute-start.9) | collective-permute-done | bytes 57376 | tf_op jit(solution)/shard_map/ppermute | solution.py:220
  44.5 1.6 %collective-permute-done.8.other_ref = f32[112,128]{1,0:T(8,128)S(1)} collective-permute-done((f32[112,128]{1,0:T(8,128)S(1)}, f32[112,128]{1,0:T(8,128)S(1)}, u32[]{:S(2)}, u32[]{:S(2)}) %collective-permute-start.8) | collective-permute-done | bytes 57376 | tf_op jit(solution)/shard_map/ppermute | solution.py:220
  46.1 1.9 %collective-permute-done.7.near_ref = f32[112,128]{1,0:T(8,128)S(1)} collective-permute-done((f32[112,128]{1,0:T(8,128)S(1)}, f32[112,128]{1,0:T(8,128)S(1)}, u32[]{:S(2)}, u32[]{:S(2)}) %collective-permute-start.7) | collective-permute-done | bytes 57376 | tf_op jit(solution)/shard_map/ppermute | solution.py:220
  48.0 5.1 %finish.1 = f32[32,128]{1,0:T(8,128)} custom-call(f32[32,128]{1,0:T(8,128)S(1)} %get-tuple-element.20.part_ref, f32[80,128]{1,0:T(8,128)S(1)} %fusion.2.gram_ref, f32[112,128]{1,0:T(8,128)S(1)} %collective-permute-done.7.near_ref, f32[112,128]{1,0:T(8,128)S(1)} %collective-permute-done.8.other_ref, f32[112,128]{1,0:T(8,128)S(1)} %collective-permute-done.9.across_ref), custom_call_target="tpu_custom_call" | custom-call | flops 1000000000 | bytes 1048576 | tf_op jit(solution)/shard_map/finish/pallas_call | solution.py:197
  (8 shorter events, 0.1 us)
Async XLA Ops:
  13.6 2.8 %collective-permute-start = (f32[2128,128]{1,0:T(8,128)S(1)}, f32[2128,128]{1,0:T(8,128)S(1)}, u32[]{:S(2)}, u32[]{:S(2)}) collective-permute-start(f32[2128,128]{1,0:T(8,128)S(1)} %pad_maximum_fusion), channel_id=1, source_target_pairs={{0,1},{1,0},{2,3},{3,2},{4,5},{5,4},{6,7},{7,6},{8,9},{9,8},{10,11... | collective-permute-start | bytes 3268616 | tf_op jit(solution)/shard_map/ppermute | solution.py:210
  16.7 8.4 %collective-permute-start.1 = (f32[592,128]{1,0:T(8,128)S(1)}, f32[592,128]{1,0:T(8,128)S(1)}, u32[]{:S(2)}, u32[]{:S(2)}) collective-permute-start(f32[592,128]{1,0:T(8,128)S(1)} %get-tuple-element.27), channel_id=1, source_target_pairs={{0,4},{1,17},{2,6},{3,19},{4,0},{5,21},{6,2},{7,23},{8,12},{9,25},... | collective-permute-start | bytes 909320 | tf_op jit(solution)/shard_map/ppermute | solution.py:220
  19.9 8.4 %collective-permute-start.2 = (f32[592,128]{1,0:T(8,128)S(1)}, f32[592,128]{1,0:T(8,128)S(1)}, u32[]{:S(2)}, u32[]{:S(2)}) collective-permute-start(f32[592,128]{1,0:T(8,128)S(1)} %get-tuple-element.28), channel_id=1, source_target_pairs={{0,6},{1,25},{2,4},{3,27},{4,2},{5,29},{6,0},{7,31},{8,14},{9,17},... | collective-permute-start | bytes 909320 | tf_op jit(solution)/shard_map/ppermute | solution.py:220
  21.0 7.5 %collective-permute-start.3 = (f32[592,128]{1,0:T(8,128)S(1)}, f32[592,128]{1,0:T(8,128)S(1)}, u32[]{:S(2)}, u32[]{:S(2)}) collective-permute-start(f32[592,128]{1,0:T(8,128)S(1)} %get-tuple-element.29), channel_id=1, source_target_pairs={{0,2},{1,9},{2,0},{3,11},{4,6},{5,13},{6,4},{7,15},{8,10},{9,1},{1... | collective-permute-start | bytes 909320 | tf_op jit(solution)/shard_map/ppermute | solution.py:220
  28.7 6.6 %collective-permute-start.4 = (f32[208,128]{1,0:T(8,128)S(1)}, f32[208,128]{1,0:T(8,128)S(1)}, u32[]{:S(2)}, u32[]{:S(2)}) collective-permute-start(f32[208,128]{1,0:T(8,128)S(1)} %get-tuple-element.24), channel_id=1, source_target_pairs={{0,16},{1,5},{2,18},{3,7},{4,20},{5,1},{6,22},{7,3},{8,24},{9,13},... | collective-permute-start | bytes 319496 | tf_op jit(solution)/shard_map/ppermute | solution.py:220
  32.7 5.9 %collective-permute-start.5 = (f32[208,128]{1,0:T(8,128)S(1)}, f32[208,128]{1,0:T(8,128)S(1)}, u32[]{:S(2)}, u32[]{:S(2)}) collective-permute-start(f32[208,128]{1,0:T(8,128)S(1)} %get-tuple-element.25), channel_id=1, source_target_pairs={{0,24},{1,7},{2,26},{3,5},{4,28},{5,3},{6,30},{7,1},{8,16},{9,15},... | collective-permute-start | bytes 319496 | tf_op jit(solution)/shard_map/ppermute | solution.py:220
  33.4 5.2 %collective-permute-start.6 = (f32[208,128]{1,0:T(8,128)S(1)}, f32[208,128]{1,0:T(8,128)S(1)}, u32[]{:S(2)}, u32[]{:S(2)}) collective-permute-start(f32[208,128]{1,0:T(8,128)S(1)} %get-tuple-element.26), channel_id=1, source_target_pairs={{0,8},{1,3},{2,10},{3,1},{4,12},{5,7},{6,14},{7,5},{8,0},{9,11},{1... | collective-permute-start | bytes 319496 | tf_op jit(solution)/shard_map/ppermute | solution.py:220
  38.7 5.8 %collective-permute-start.9 = (f32[112,128]{1,0:T(8,128)S(1)}, f32[112,128]{1,0:T(8,128)S(1)}, u32[]{:S(2)}, u32[]{:S(2)}) collective-permute-start(f32[112,128]{1,0:T(8,128)S(1)} %get-tuple-element.21), channel_id=1, source_target_pairs={{0,64},{1,65},{2,66},{3,67},{4,68},{5,69},{6,70},{7,71},{8,72},{9,... | collective-permute-start | bytes 172040 | tf_op jit(solution)/shard_map/ppermute | solution.py:220
  41.9 4.2 %collective-permute-start.8 = (f32[112,128]{1,0:T(8,128)S(1)}, f32[112,128]{1,0:T(8,128)S(1)}, u32[]{:S(2)}, u32[]{:S(2)}) collective-permute-start(f32[112,128]{1,0:T(8,128)S(1)} %get-tuple-element.22), channel_id=1, source_target_pairs={{0,32},{1,33},{2,34},{3,35},{4,36},{5,37},{6,38},{7,39},{8,40},{9,... | collective-permute-start | bytes 172040 | tf_op jit(solution)/shard_map/ppermute | solution.py:220
  42.6 5.4 %collective-permute-start.7 = (f32[112,128]{1,0:T(8,128)S(1)}, f32[112,128]{1,0:T(8,128)S(1)}, u32[]{:S(2)}, u32[]{:S(2)}) collective-permute-start(f32[112,128]{1,0:T(8,128)S(1)} %get-tuple-element.23), channel_id=1, source_target_pairs={{0,96},{1,97},{2,98},{3,99},{4,100},{5,101},{6,102},{7,103},{8,104... | collective-permute-start | bytes 172040 | tf_op jit(solution)/shard_map/ppermute | solution.py:220

commit v6 on v5

--- a/solution.py
+++ b/solution.py
@@ -91,7 +91,7 @@
             even, odd = tile[chip, 0], tile[chip, 1]
             by_y, by_z, by_x = turn(to_y, y), turn(to_z, z), turn(to_x, x)
             even_at = by_x, SIDE * by_z + by_y
-            odd_at = by_z, SIDE * by_x + by_y
+            odd_at = by_z, SIDE * by_y + by_x
             mine_at = [jnp.where(first, p, q) for p, q in zip(even_at, odd_at)]
             other_at = [jnp.where(first, q, p) for p, q in zip(even_at, odd_at)]
             mine_ref[mine_at[0], mine_at[1]] = jnp.where(first, even, odd)
@@ -124,7 +124,7 @@
     )(place, slab, omega)
 
 
-AXES = (2, 1), (1, 2), (0, 0)
+AXES = (2, 1), (1, 0), (0, 2)
 MASKS = 3, 1, 2
 
 
@@ -227,18 +227,20 @@
     test_matrix = pltpu.with_memory_space_constraint(test_matrix, pltpu.HBM)
     gram, mine, other = sketch_call(place, slab, test_matrix)
 
-    rows = SIDE**3 * 32
-    mine, other = mine.reshape(rows, K), other.reshape(rows, K)
-    got = swap_cores(jnp.concatenate([other, gram]))
-    part, gram = mine + got[:rows], gram + got[rows:]
+    rows = SIDE**2 * 32
+    mine, other = mine.reshape(SIDE, rows, K), other.reshape(SIDE, rows, K)
+    got = swap_cores(jnp.concatenate([other[3], gram]))
+    parts = [mine[i] + swap_cores(other[i]) for i in range(3)] + [mine[3] + got[:rows]]
+    gram = gram + got[rows:]
     for number, axes in enumerate(AXES):
-        rows //= 4
-        stay, *leave = (part[i * rows : (i + 1) * rows] for i in range(4))
+        stay, *leave = parts
         got = [swap_chips(jnp.concatenate([piece, gram]), axes, mask) for piece, mask in zip(leave, MASKS)]
         if number + 1 == len(AXES):
             return finish_call(stay, gram, got).T
         part = (stay + got[2][:rows]) + (got[0][:rows] + got[1][:rows])
         gram = (gram + got[2][rows:]) + (got[0][rows:] + got[1][rows:])
+        rows //= 4
+        parts = [part[i * rows : (i + 1) * rows] for i in range(4)]
 
 
 def solution(mesh):

time: 53.2 us -> 52.7 us (level)
  waiting for transfers between devices: 20.1 us -> 18.6 us
  starting transfers between devices: 13.7 us -> 14.7 us
    ppermute x9, waiting for transfers between devices: 17.4 us -> 15.9 us  [swap_chips(): return lax.ppermute(array, 'rows', pairs)]
    ppermute x1 -> x4, starting transfers between devices: 0.09 us -> 1.06 us  [swap_cores(): lax.ppermute(array, 'rows', [(i, i ^ 1) for i in range(2 * SIDE ** 3)])]
    ppermute x1 -> x4, waiting for transfers between devices: 2.71 us -> 2.71 us  [swap_cores(): lax.ppermute(array, 'rows', [(i, i ^ 1) for i in range(2 * SIDE ** 3)])]
  transfers between devices with their start and end apart: 10 -> 13, of which waited for: 9 -> 12; matrix products, arithmetic and copies ran while one was open for 0% -> 0% of each run, Pallas kernels for 0% -> 0%
where the time goes in v6:
time: 52.7 us; the launch traced here: 52.6 us
  Pallas kernels  18.6 us (35%)
  waiting for transfers between devices  18.6 us (35%)
  starting transfers between devices  14.7 us (28%)
    ppermute x9, waiting for transfers between devices, swap_chips(): return lax.ppermute(array, 'rows', pairs)  15.9 us
    ppermute x9, starting transfers between devices, swap_chips(): return lax.ppermute(array, 'rows', pairs)  13.6 us
    pallas_call x1, Pallas kernels, sketch_call(): pl.pallas_call(sketch_kernel, out_shape=(jax.ShapeDtypeStruct((80, K), jn...  13.5 us
    pallas_call x1, Pallas kernels, finish_call(): pl.pallas_call(finish_kernel, out_shape=jax.ShapeDtypeStruct(part.shape,...  5.12 us
    ppermute x4, waiting for transfers between devices, swap_cores(): lax.ppermute(array, 'rows', [(i, i ^ 1) for i in range(2 * SIDE ** 3)])  2.71 us
    ppermute x4, starting transfers between devices, swap_cores(): lax.ppermute(array, 'rows', [(i, i ^ 1) for i in range(2 * SIDE ** 3)])  1.06 us
  transfers between devices with their start and end apart: 13, of which 12 were waited for; matrix products, arithmetic and copies ran while one was open for 0% of the time, Pallas kernels for 0%

profile of v6, /device:TPU:0, one launch (start us, length us, event | category | flops | bytes accessed | tf_op | source)
XLA Modules:
  0.0 52.6 jit_solution(9272871186067955930)
XLA Ops:
  0.0 0.1 pad_add_fusion.place_ref
  0.1 13.5 %sketch.1 = (f32[80,128]{1,0:T(8,128)S(1)}, f32[4,16,32,128]{3,2,1,0:T(8,128)S(1)}, f32[4,16,32,128]{3,2,1,0:T(8,128)S(1)}) custom-call(s32[4]{0:T(128)S(1)} %pad_add_fusion.place_ref, bf16[2048,4096]{1,0:T(8,128)(2,1)} %slab_ref.1, bf16[4096,128]{1,0:T(8,128)(2,1)} %omega_ref.1), custom_call_target="tpu_custom_call" | custom-call | flops 6442450944 | bytes 16777216 | tf_op jit(solution)/shard_map/sketch/pallas_call | solution.py:106
  13.5 0.1 fusion.5
  13.6 0.1 collective-permute-start.5
  13.7 0.5 collective-permute-start.3
  14.2 0.2 collective-permute-start.1
  14.4 0.1 fusion.4
  14.5 0.8 %collective-permute-done.5 = f32[512,128]{1,0:T(8,128)S(1)} collective-permute-done((f32[512,128]{1,0:T(8,128)S(1)}, f32[512,128]{1,0:T(8,128)S(1)}, u32[]{:S(2)}, u32[]{:S(2)}) %collective-permute-start.5) | collective-permute-done | bytes 262176 | tf_op jit(solution)/shard_map/ppermute | solution.py:210
  15.3 0.3 collective-permute-done.3
  15.7 0.4 collective-permute-done.1
  16.1 0.1 pad_maximum_fusion.2
  16.2 3.2 %collective-permute-start.2 = (f32[592,128]{1,0:T(8,128)S(1)}, f32[592,128]{1,0:T(8,128)S(1)}, u32[]{:S(2)}, u32[]{:S(2)}) collective-permute-start(f32[592,128]{1,0:T(8,128)S(1)} %get-tuple-element.32), channel_id=1, source_target_pairs={{0,4},{1,17},{2,6},{3,19},{4,0},{5,21},{6,2},{7,23},{8,12},{9,25},... | collective-permute-start | bytes 909320 | tf_op jit(solution)/shard_map/ppermute | solution.py:220
  19.4 1.1 %collective-permute-start.4 = (f32[592,128]{1,0:T(8,128)S(1)}, f32[592,128]{1,0:T(8,128)S(1)}, u32[]{:S(2)}, u32[]{:S(2)}) collective-permute-start(f32[592,128]{1,0:T(8,128)S(1)} %get-tuple-element.33), channel_id=1, source_target_pairs={{0,6},{1,25},{2,4},{3,27},{4,2},{5,29},{6,0},{7,31},{8,14},{9,17},... | collective-permute-start | bytes 909320 | tf_op jit(solution)/shard_map/ppermute | solution.py:220
  20.5 0.0 collective-permute-start.6
  20.5 0.3 collective-permute-start
  20.8 1.2 %collective-permute-done = f32[512,128]{1,0:T(8,128)S(1)} collective-permute-done((f32[512,128]{1,0:T(8,128)S(1)}, f32[512,128]{1,0:T(8,128)S(1)}, u32[]{:S(2)}, u32[]{:S(2)}) %collective-permute-start) | collective-permute-done | bytes 262176 | tf_op jit(solution)/shard_map/ppermute | solution.py:210
  22.0 2.6 %collective-permute-done.2 = f32[592,128]{1,0:T(8,128)S(1)} collective-permute-done((f32[592,128]{1,0:T(8,128)S(1)}, f32[592,128]{1,0:T(8,128)S(1)}, u32[]{:S(2)}, u32[]{:S(2)}) %collective-permute-start.2) | collective-permute-done | bytes 303136 | tf_op jit(solution)/shard_map/ppermute | solution.py:220
  24.6 3.2 %collective-permute-done.4 = f32[592,128]{1,0:T(8,128)S(1)} collective-permute-done((f32[592,128]{1,0:T(8,128)S(1)}, f32[592,128]{1,0:T(8,128)S(1)}, u32[]{:S(2)}, u32[]{:S(2)}) %collective-permute-start.4) | collective-permute-done | bytes 303136 | tf_op jit(solution)/shard_map/ppermute | solution.py:220
  27.8 0.2 collective-permute-done.6
  28.0 0.1 fusion
  28.2 4.0 %collective-permute-start.7 = (f32[208,128]{1,0:T(8,128)S(1)}, f32[208,128]{1,0:T(8,128)S(1)}, u32[]{:S(2)}, u32[]{:S(2)}) collective-permute-start(f32[208,128]{1,0:T(8,128)S(1)} %get-tuple-element.29), channel_id=1, source_target_pairs={{0,16},{1,65},{2,18},{3,67},{4,20},{5,69},{6,22},{7,71},{8,24},{9,... | collective-permute-start | bytes 319496 | tf_op jit(solution)/shard_map/ppermute | solution.py:220
  32.2 0.7 %collective-permute-start.8 = (f32[208,128]{1,0:T(8,128)S(1)}, f32[208,128]{1,0:T(8,128)S(1)}, u32[]{:S(2)}, u32[]{:S(2)}) collective-permute-start(f32[208,128]{1,0:T(8,128)S(1)} %get-tuple-element.30), channel_id=1, source_target_pairs={{0,24},{1,97},{2,26},{3,99},{4,28},{5,101},{6,30},{7,103},{8,16},{... | collective-permute-start | bytes 319496 | tf_op jit(solution)/shard_map/ppermute | solution.py:220
  32.9 0.3 collective-permute-start.9
  33.2 1.7 %collective-permute-done.7 = f32[208,128]{1,0:T(8,128)S(1)} collective-permute-done((f32[208,128]{1,0:T(8,128)S(1)}, f32[208,128]{1,0:T(8,128)S(1)}, u32[]{:S(2)}, u32[]{:S(2)}) %collective-permute-start.7) | collective-permute-done | bytes 106528 | tf_op jit(solution)/shard_map/ppermute | solution.py:220
  34.8 3.2 %collective-permute-done.8 = f32[208,128]{1,0:T(8,128)S(1)} collective-permute-done((f32[208,128]{1,0:T(8,128)S(1)}, f32[208,128]{1,0:T(8,128)S(1)}, u32[]{:S(2)}, u32[]{:S(2)}) %collective-permute-start.8) | collective-permute-done | bytes 106528 | tf_op jit(solution)/shard_map/ppermute | solution.py:220
  38.1 0.0 collective-permute-done.9
  38.2 3.3 %collective-permute-start.12 = (f32[112,128]{1,0:T(8,128)S(1)}, f32[112,128]{1,0:T(8,128)S(1)}, u32[]{:S(2)}, u32[]{:S(2)}) collective-permute-start(f32[112,128]{1,0:T(8,128)S(1)} %get-tuple-element.26), channel_id=1, source_target_pairs={{0,64},{1,5},{2,66},{3,7},{4,68},{5,1},{6,70},{7,3},{8,72},{9,13},... | collective-permute-start | bytes 172040 | tf_op jit(solution)/shard_map/ppermute | solution.py:220
  41.4 0.7 %collective-permute-start.11 = (f32[112,128]{1,0:T(8,128)S(1)}, f32[112,128]{1,0:T(8,128)S(1)}, u32[]{:S(2)}, u32[]{:S(2)}) collective-permute-start(f32[112,128]{1,0:T(8,128)S(1)} %get-tuple-element.27), channel_id=1, source_target_pairs={{0,32},{1,3},{2,34},{3,1},{4,36},{5,7},{6,38},{7,5},{8,40},{9,11},... | collective-permute-start | bytes 172040 | tf_op jit(solution)/shard_map/ppermute | solution.py:220
  42.1 0.4 collective-permute-start.10
  42.5 1.4 %collective-permute-done.12.across_ref = f32[112,128]{1,0:T(8,128)S(1)} collective-permute-done((f32[112,128]{1,0:T(8,128)S(1)}, f32[112,128]{1,0:T(8,128)S(1)}, u32[]{:S(2)}, u32[]{:S(2)}) %collective-permute-start.12) | collective-permute-done | bytes 57376 | tf_op jit(solution)/shard_map/ppermute | solution.py:220
  43.9 1.7 %collective-permute-done.11.other_ref = f32[112,128]{1,0:T(8,128)S(1)} collective-permute-done((f32[112,128]{1,0:T(8,128)S(1)}, f32[112,128]{1,0:T(8,128)S(1)}, u32[]{:S(2)}, u32[]{:S(2)}) %collective-permute-start.11) | collective-permute-done | bytes 57376 | tf_op jit(solution)/shard_map/ppermute | solution.py:220
  45.6 1.9 %collective-permute-done.10.near_ref = f32[112,128]{1,0:T(8,128)S(1)} collective-permute-done((f32[112,128]{1,0:T(8,128)S(1)}, f32[112,128]{1,0:T(8,128)S(1)}, u32[]{:S(2)}, u32[]{:S(2)}) %collective-permute-start.10) | collective-permute-done | bytes 57376 | tf_op jit(solution)/shard_map/ppermute | solution.py:220
  47.5 5.1 %finish.1 = f32[32,128]{1,0:T(8,128)} custom-call(f32[32,128]{1,0:T(8,128)S(1)} %get-tuple-element.25.part_ref, f32[80,128]{1,0:T(8,128)S(1)} %fusion.2.gram_ref, f32[112,128]{1,0:T(8,128)S(1)} %collective-permute-done.10.near_ref, f32[112,128]{1,0:T(8,128)S(1)} %collective-permute-done.11.other_ref, f32[112,128]{1,0:T(8,128)S(1)} %collective-permute-done.12.across_ref), custom_call_target="tpu_custom_call" | custom-call | flops 1000000000 | bytes 1048576 | tf_op jit(solution)/shard_map/finish/pallas_call | solution.py:197
  (12 shorter events, 0.2 us)
Async XLA Ops:
  13.6 1.6 %collective-permute-start.5 = (f32[512,128]{1,0:T(8,128)S(1)}, f32[512,128]{1,0:T(8,128)S(1)}, u32[]{:S(2)}, u32[]{:S(2)}) collective-permute-start(f32[512,128]{1,0:T(8,128)S(1)} %bitcast.22), channel_id=1, source_target_pairs={{0,1},{1,0},{2,3},{3,2},{4,5},{5,4},{6,7},{7,6},{8,9},{9,8},{10,11... | collective-permute-start | bytes 786440 | tf_op jit(solution)/shard_map/ppermute | solution.py:210
  13.7 1.9 %collective-permute-start.3 = (f32[512,128]{1,0:T(8,128)S(1)}, f32[512,128]{1,0:T(8,128)S(1)}, u32[]{:S(2)}, u32[]{:S(2)}) collective-permute-start(f32[512,128]{1,0:T(8,128)S(1)} %bitcast.21), channel_id=1, source_target_pairs={{0,1},{1,0},{2,3},{3,2},{4,5},{5,4},{6,7},{7,6},{8,9},{9,8},{10,11... | collective-permute-start | bytes 786440 | tf_op jit(solution)/shard_map/ppermute | solution.py:210
  14.2 1.8 %collective-permute-start.1 = (f32[592,128]{1,0:T(8,128)S(1)}, f32[592,128]{1,0:T(8,128)S(1)}, u32[]{:S(2)}, u32[]{:S(2)}) collective-permute-start(f32[592,128]{1,0:T(8,128)S(1)} %pad_maximum_fusion.3), channel_id=1, source_target_pairs={{0,1},{1,0},{2,3},{3,2},{4,5},{5,4},{6,7},{7,6},{8,9},{9,8},{10,11... | collective-permute-start | bytes 909320 | tf_op jit(solution)/shard_map/ppermute | solution.py:210
  16.2 8.4 %collective-permute-start.2 = (f32[592,128]{1,0:T(8,128)S(1)}, f32[592,128]{1,0:T(8,128)S(1)}, u32[]{:S(2)}, u32[]{:S(2)}) collective-permute-start(f32[592,128]{1,0:T(8,128)S(1)} %get-tuple-element.32), channel_id=1, source_target_pairs={{0,4},{1,17},{2,6},{3,19},{4,0},{5,21},{6,2},{7,23},{8,12},{9,25},... | collective-permute-start | bytes 909320 | tf_op jit(solution)/shard_map/ppermute | solution.py:220
  19.4 8.4 %collective-permute-start.4 = (f32[592,128]{1,0:T(8,128)S(1)}, f32[592,128]{1,0:T(8,128)S(1)}, u32[]{:S(2)}, u32[]{:S(2)}) collective-permute-start(f32[592,128]{1,0:T(8,128)S(1)} %get-tuple-element.33), channel_id=1, source_target_pairs={{0,6},{1,25},{2,4},{3,27},{4,2},{5,29},{6,0},{7,31},{8,14},{9,17},... | collective-permute-start | bytes 909320 | tf_op jit(solution)/shard_map/ppermute | solution.py:220
  20.5 7.5 %collective-permute-start.6 = (f32[592,128]{1,0:T(8,128)S(1)}, f32[592,128]{1,0:T(8,128)S(1)}, u32[]{:S(2)}, u32[]{:S(2)}) collective-permute-start(f32[592,128]{1,0:T(8,128)S(1)} %get-tuple-element.34), channel_id=1, source_target_pairs={{0,2},{1,9},{2,0},{3,11},{4,6},{5,13},{6,4},{7,15},{8,10},{9,1},{1... | collective-permute-start | bytes 909320 | tf_op jit(solution)/shard_map/ppermute | solution.py:220
  20.5 1.5 %collective-permute-start = (f32[512,128]{1,0:T(8,128)S(1)}, f32[512,128]{1,0:T(8,128)S(1)}, u32[]{:S(2)}, u32[]{:S(2)}) collective-permute-start(f32[512,128]{1,0:T(8,128)S(1)} %bitcast.20), channel_id=1, source_target_pairs={{0,1},{1,0},{2,3},{3,2},{4,5},{5,4},{6,7},{7,6},{8,9},{9,8},{10,11... | collective-permute-start | bytes 786440 | tf_op jit(solution)/shard_map/ppermute | solution.py:210
  28.2 6.6 %collective-permute-start.7 = (f32[208,128]{1,0:T(8,128)S(1)}, f32[208,128]{1,0:T(8,128)S(1)}, u32[]{:S(2)}, u32[]{:S(2)}) collective-permute-start(f32[208,128]{1,0:T(8,128)S(1)} %get-tuple-element.29), channel_id=1, source_target_pairs={{0,16},{1,65},{2,18},{3,67},{4,20},{5,69},{6,22},{7,71},{8,24},{9,... | collective-permute-start | bytes 319496 | tf_op jit(solution)/shard_map/ppermute | solution.py:220
  32.2 5.9 %collective-permute-start.8 = (f32[208,128]{1,0:T(8,128)S(1)}, f32[208,128]{1,0:T(8,128)S(1)}, u32[]{:S(2)}, u32[]{:S(2)}) collective-permute-start(f32[208,128]{1,0:T(8,128)S(1)} %get-tuple-element.30), channel_id=1, source_target_pairs={{0,24},{1,97},{2,26},{3,99},{4,28},{5,101},{6,30},{7,103},{8,16},{... | collective-permute-start | bytes 319496 | tf_op jit(solution)/shard_map/ppermute | solution.py:220
  32.9 5.2 %collective-permute-start.9 = (f32[208,128]{1,0:T(8,128)S(1)}, f32[208,128]{1,0:T(8,128)S(1)}, u32[]{:S(2)}, u32[]{:S(2)}) collective-permute-start(f32[208,128]{1,0:T(8,128)S(1)} %get-tuple-element.31), channel_id=1, source_target_pairs={{0,8},{1,33},{2,10},{3,35},{4,12},{5,37},{6,14},{7,39},{8,0},{9,41... | collective-permute-start | bytes 319496 | tf_op jit(solution)/shard_map/ppermute | solution.py:220
  38.2 5.8 %collective-permute-start.12 = (f32[112,128]{1,0:T(8,128)S(1)}, f32[112,128]{1,0:T(8,128)S(1)}, u32[]{:S(2)}, u32[]{:S(2)}) collective-permute-start(f32[112,128]{1,0:T(8,128)S(1)} %get-tuple-element.26), channel_id=1, source_target_pairs={{0,64},{1,5},{2,66},{3,7},{4,68},{5,1},{6,70},{7,3},{8,72},{9,13},... | collective-permute-start | bytes 172040 | tf_op jit(solution)/shard_map/ppermute | solution.py:220
  41.4 4.2 %collective-permute-start.11 = (f32[112,128]{1,0:T(8,128)S(1)}, f32[112,128]{1,0:T(8,128)S(1)}, u32[]{:S(2)}, u32[]{:S(2)}) collective-permute-start(f32[112,128]{1,0:T(8,128)S(1)} %get-tuple-element.27), channel_id=1, source_target_pairs={{0,32},{1,3},{2,34},{3,1},{4,36},{5,7},{6,38},{7,5},{8,40},{9,11},... | collective-permute-start | bytes 172040 | tf_op jit(solution)/shard_map/ppermute | solution.py:220
  42.1 5.4 %collective-permute-start.10 = (f32[112,128]{1,0:T(8,128)S(1)}, f32[112,128]{1,0:T(8,128)S(1)}, u32[]{:S(2)}, u32[]{:S(2)}) collective-permute-start(f32[112,128]{1,0:T(8,128)S(1)} %get-tuple-element.28), channel_id=1, source_target_pairs={{0,96},{1,7},{2,98},{3,5},{4,100},{5,3},{6,102},{7,1},{8,104},{9,1... | collective-permute-start | bytes 172040 | tf_op jit(solution)/shard_map/ppermute | solution.py:220

commit v7 on v6

--- a/solution.py
+++ b/solution.py
@@ -90,8 +90,8 @@
             to_y, to_z, to_x = place_of(n * (COLS // 64) + chip)
             even, odd = tile[chip, 0], tile[chip, 1]
             by_y, by_z, by_x = turn(to_y, y), turn(to_z, z), turn(to_x, x)
-            even_at = by_x, SIDE * by_z + by_y
-            odd_at = by_z, SIDE * by_y + by_x
+            even_at = by_x, SIDE * by_y + by_z
+            odd_at = by_z, SIDE * by_x + by_y
             mine_at = [jnp.where(first, p, q) for p, q in zip(even_at, odd_at)]
             other_at = [jnp.where(first, q, p) for p, q in zip(even_at, odd_at)]
             mine_ref[mine_at[0], mine_at[1]] = jnp.where(first, even, odd)
@@ -124,7 +124,7 @@
     )(place, slab, omega)
 
 
-AXES = (2, 1), (1, 0), (0, 2)
+AXES = (2, 1), (0, 2), (1, 0)
 MASKS = 3, 1, 2
 
 

time: 52.7 us -> 53.1 us (level)
  no operation moved by 1% of the time
where the time goes in v7:
time: 53.1 us; the launch traced here: 53 us
  waiting for transfers between devices  18.9 us (36%)
  Pallas kernels  18.6 us (35%)
  starting transfers between devices  14.7 us (28%)
    ppermute x9, waiting for transfers between devices, swap_chips(): return lax.ppermute(array, 'rows', pairs)  16.2 us
    ppermute x9, starting transfers between devices, swap_chips(): return lax.ppermute(array, 'rows', pairs)  13.6 us
    pallas_call x1, Pallas kernels, sketch_call(): pl.pallas_call(sketch_kernel, out_shape=(jax.ShapeDtypeStruct((80, K), jn...  13.5 us
    pallas_call x1, Pallas kernels, finish_call(): pl.pallas_call(finish_kernel, out_shape=jax.ShapeDtypeStruct(part.shape,...  5.12 us
    ppermute x4, waiting for transfers between devices, swap_cores(): lax.ppermute(array, 'rows', [(i, i ^ 1) for i in range(2 * SIDE ** 3)])  2.71 us
    ppermute x4, starting transfers between devices, swap_cores(): lax.ppermute(array, 'rows', [(i, i ^ 1) for i in range(2 * SIDE ** 3)])  1.06 us
  transfers between devices with their start and end apart: 13, of which 12 were waited for; matrix products, arithmetic and copies ran while one was open for 0% of the time, Pallas kernels for 0%

profile of v7, /device:TPU:0, one launch (start us, length us, event | category | flops | bytes accessed | tf_op | source)
XLA Modules:
  0.0 53.0 jit_solution(6200466798154118065)
XLA Ops:
  0.0 0.1 pad_add_fusion.place_ref
  0.1 13.5 %sketch.1 = (f32[80,128]{1,0:T(8,128)S(1)}, f32[4,16,32,128]{3,2,1,0:T(8,128)S(1)}, f32[4,16,32,128]{3,2,1,0:T(8,128)S(1)}) custom-call(s32[4]{0:T(128)S(1)} %pad_add_fusion.place_ref, bf16[2048,4096]{1,0:T(8,128)(2,1)} %slab_ref.1, bf16[4096,128]{1,0:T(8,128)(2,1)} %omega_ref.1), custom_call_target="tpu_custom_call" | custom-call | flops 6442450944 | bytes 16777216 | tf_op jit(solution)/shard_map/sketch/pallas_call | solution.py:106
  13.5 0.1 fusion.5
  13.6 0.1 collective-permute-start.5
  13.7 0.5 collective-permute-start.3
  14.2 0.2 collective-permute-start.1
  14.4 0.1 fusion.4
  14.5 0.8 %collective-permute-done.5 = f32[512,128]{1,0:T(8,128)S(1)} collective-permute-done((f32[512,128]{1,0:T(8,128)S(1)}, f32[512,128]{1,0:T(8,128)S(1)}, u32[]{:S(2)}, u32[]{:S(2)}) %collective-permute-start.5) | collective-permute-done | bytes 262176 | tf_op jit(solution)/shard_map/ppermute | solution.py:210
  15.3 0.3 collective-permute-done.3
  15.7 0.4 collective-permute-done.1
  16.1 0.1 pad_maximum_fusion.2
  16.2 3.2 %collective-permute-start.2 = (f32[592,128]{1,0:T(8,128)S(1)}, f32[592,128]{1,0:T(8,128)S(1)}, u32[]{:S(2)}, u32[]{:S(2)}) collective-permute-start(f32[592,128]{1,0:T(8,128)S(1)} %get-tuple-element.32), channel_id=1, source_target_pairs={{0,4},{1,17},{2,6},{3,19},{4,0},{5,21},{6,2},{7,23},{8,12},{9,25},... | collective-permute-start | bytes 909320 | tf_op jit(solution)/shard_map/ppermute | solution.py:220
  19.4 1.1 %collective-permute-start.4 = (f32[592,128]{1,0:T(8,128)S(1)}, f32[592,128]{1,0:T(8,128)S(1)}, u32[]{:S(2)}, u32[]{:S(2)}) collective-permute-start(f32[592,128]{1,0:T(8,128)S(1)} %get-tuple-element.33), channel_id=1, source_target_pairs={{0,6},{1,25},{2,4},{3,27},{4,2},{5,29},{6,0},{7,31},{8,14},{9,17},... | collective-permute-start | bytes 909320 | tf_op jit(solution)/shard_map/ppermute | solution.py:220
  20.5 0.0 collective-permute-start.6
  20.5 0.3 collective-permute-start
  20.8 1.2 %collective-permute-done = f32[512,128]{1,0:T(8,128)S(1)} collective-permute-done((f32[512,128]{1,0:T(8,128)S(1)}, f32[512,128]{1,0:T(8,128)S(1)}, u32[]{:S(2)}, u32[]{:S(2)}) %collective-permute-start) | collective-permute-done | bytes 262176 | tf_op jit(solution)/shard_map/ppermute | solution.py:210
  22.0 2.6 %collective-permute-done.2 = f32[592,128]{1,0:T(8,128)S(1)} collective-permute-done((f32[592,128]{1,0:T(8,128)S(1)}, f32[592,128]{1,0:T(8,128)S(1)}, u32[]{:S(2)}, u32[]{:S(2)}) %collective-permute-start.2) | collective-permute-done | bytes 303136 | tf_op jit(solution)/shard_map/ppermute | solution.py:220
  24.6 3.2 %collective-permute-done.4 = f32[592,128]{1,0:T(8,128)S(1)} collective-permute-done((f32[592,128]{1,0:T(8,128)S(1)}, f32[592,128]{1,0:T(8,128)S(1)}, u32[]{:S(2)}, u32[]{:S(2)}) %collective-permute-start.4) | collective-permute-done | bytes 303136 | tf_op jit(solution)/shard_map/ppermute | solution.py:220
  27.8 0.2 collective-permute-done.6
  28.0 0.1 fusion
  28.2 3.3 %collective-permute-start.7 = (f32[208,128]{1,0:T(8,128)S(1)}, f32[208,128]{1,0:T(8,128)S(1)}, u32[]{:S(2)}, u32[]{:S(2)}) collective-permute-start(f32[208,128]{1,0:T(8,128)S(1)} %get-tuple-element.29), channel_id=1, source_target_pairs={{0,64},{1,5},{2,66},{3,7},{4,68},{5,1},{6,70},{7,3},{8,72},{9,13},... | collective-permute-start | bytes 319496 | tf_op jit(solution)/shard_map/ppermute | solution.py:220
  31.5 1.1 %collective-permute-start.8 = (f32[208,128]{1,0:T(8,128)S(1)}, f32[208,128]{1,0:T(8,128)S(1)}, u32[]{:S(2)}, u32[]{:S(2)}) collective-permute-start(f32[208,128]{1,0:T(8,128)S(1)} %get-tuple-element.30), channel_id=1, source_target_pairs={{0,96},{1,7},{2,98},{3,5},{4,100},{5,3},{6,102},{7,1},{8,104},{9,1... | collective-permute-start | bytes 319496 | tf_op jit(solution)/shard_map/ppermute | solution.py:220
  32.5 0.0 collective-permute-start.9
  32.5 2.0 %collective-permute-done.7 = f32[208,128]{1,0:T(8,128)S(1)} collective-permute-done((f32[208,128]{1,0:T(8,128)S(1)}, f32[208,128]{1,0:T(8,128)S(1)}, u32[]{:S(2)}, u32[]{:S(2)}) %collective-permute-start.7) | collective-permute-done | bytes 106528 | tf_op jit(solution)/shard_map/ppermute | solution.py:220
  34.5 2.9 %collective-permute-done.8 = f32[208,128]{1,0:T(8,128)S(1)} collective-permute-done((f32[208,128]{1,0:T(8,128)S(1)}, f32[208,128]{1,0:T(8,128)S(1)}, u32[]{:S(2)}, u32[]{:S(2)}) %collective-permute-start.8) | collective-permute-done | bytes 106528 | tf_op jit(solution)/shard_map/ppermute | solution.py:220
  37.4 0.0 collective-permute-done.9
  37.5 4.0 %collective-permute-start.12 = (f32[112,128]{1,0:T(8,128)S(1)}, f32[112,128]{1,0:T(8,128)S(1)}, u32[]{:S(2)}, u32[]{:S(2)}) collective-permute-start(f32[112,128]{1,0:T(8,128)S(1)} %get-tuple-element.26), channel_id=1, source_target_pairs={{0,16},{1,65},{2,18},{3,67},{4,20},{5,69},{6,22},{7,71},{8,24},{9,... | collective-permute-start | bytes 172040 | tf_op jit(solution)/shard_map/ppermute | solution.py:220
  41.4 1.0 %collective-permute-start.11 = (f32[112,128]{1,0:T(8,128)S(1)}, f32[112,128]{1,0:T(8,128)S(1)}, u32[]{:S(2)}, u32[]{:S(2)}) collective-permute-start(f32[112,128]{1,0:T(8,128)S(1)} %get-tuple-element.27), channel_id=1, source_target_pairs={{0,8},{1,33},{2,10},{3,35},{4,12},{5,37},{6,14},{7,39},{8,0},{9,41... | collective-permute-start | bytes 172040 | tf_op jit(solution)/shard_map/ppermute | solution.py:220
  42.5 0.0 collective-permute-start.10
  42.5 1.1 %collective-permute-done.12.across_ref = f32[112,128]{1,0:T(8,128)S(1)} collective-permute-done((f32[112,128]{1,0:T(8,128)S(1)}, f32[112,128]{1,0:T(8,128)S(1)}, u32[]{:S(2)}, u32[]{:S(2)}) %collective-permute-start.12) | collective-permute-done | bytes 57376 | tf_op jit(solution)/shard_map/ppermute | solution.py:220
  43.6 2.0 %collective-permute-done.11.other_ref = f32[112,128]{1,0:T(8,128)S(1)} collective-permute-done((f32[112,128]{1,0:T(8,128)S(1)}, f32[112,128]{1,0:T(8,128)S(1)}, u32[]{:S(2)}, u32[]{:S(2)}) %collective-permute-start.11) | collective-permute-done | bytes 57376 | tf_op jit(solution)/shard_map/ppermute | solution.py:220
  45.6 2.2 %collective-permute-done.10.near_ref = f32[112,128]{1,0:T(8,128)S(1)} collective-permute-done((f32[112,128]{1,0:T(8,128)S(1)}, f32[112,128]{1,0:T(8,128)S(1)}, u32[]{:S(2)}, u32[]{:S(2)}) %collective-permute-start.10) | collective-permute-done | bytes 57376 | tf_op jit(solution)/shard_map/ppermute | solution.py:220
  47.8 5.1 %finish.1 = f32[32,128]{1,0:T(8,128)} custom-call(f32[32,128]{1,0:T(8,128)S(1)} %get-tuple-element.25.part_ref, f32[80,128]{1,0:T(8,128)S(1)} %fusion.2.gram_ref, f32[112,128]{1,0:T(8,128)S(1)} %collective-permute-done.10.near_ref, f32[112,128]{1,0:T(8,128)S(1)} %collective-permute-done.11.other_ref, f32[112,128]{1,0:T(8,128)S(1)} %collective-permute-done.12.across_ref), custom_call_target="tpu_custom_call" | custom-call | flops 1000000000 | bytes 1048576 | tf_op jit(solution)/shard_map/finish/pallas_call | solution.py:197
  (12 shorter events, 0.2 us)
Async XLA Ops:
  13.6 1.6 %collective-permute-start.5 = (f32[512,128]{1,0:T(8,128)S(1)}, f32[512,128]{1,0:T(8,128)S(1)}, u32[]{:S(2)}, u32[]{:S(2)}) collective-permute-start(f32[512,128]{1,0:T(8,128)S(1)} %bitcast.22), channel_id=1, source_target_pairs={{0,1},{1,0},{2,3},{3,2},{4,5},{5,4},{6,7},{7,6},{8,9},{9,8},{10,11... | collective-permute-start | bytes 786440 | tf_op jit(solution)/shard_map/ppermute | solution.py:210
  13.7 1.9 %collective-permute-start.3 = (f32[512,128]{1,0:T(8,128)S(1)}, f32[512,128]{1,0:T(8,128)S(1)}, u32[]{:S(2)}, u32[]{:S(2)}) collective-permute-start(f32[512,128]{1,0:T(8,128)S(1)} %bitcast.21), channel_id=1, source_target_pairs={{0,1},{1,0},{2,3},{3,2},{4,5},{5,4},{6,7},{7,6},{8,9},{9,8},{10,11... | collective-permute-start | bytes 786440 | tf_op jit(solution)/shard_map/ppermute | solution.py:210
  14.2 1.8 %collective-permute-start.1 = (f32[592,128]{1,0:T(8,128)S(1)}, f32[592,128]{1,0:T(8,128)S(1)}, u32[]{:S(2)}, u32[]{:S(2)}) collective-permute-start(f32[592,128]{1,0:T(8,128)S(1)} %pad_maximum_fusion.3), channel_id=1, source_target_pairs={{0,1},{1,0},{2,3},{3,2},{4,5},{5,4},{6,7},{7,6},{8,9},{9,8},{10,11... | collective-permute-start | bytes 909320 | tf_op jit(solution)/shard_map/ppermute | solution.py:210
  16.2 8.4 %collective-permute-start.2 = (f32[592,128]{1,0:T(8,128)S(1)}, f32[592,128]{1,0:T(8,128)S(1)}, u32[]{:S(2)}, u32[]{:S(2)}) collective-permute-start(f32[592,128]{1,0:T(8,128)S(1)} %get-tuple-element.32), channel_id=1, source_target_pairs={{0,4},{1,17},{2,6},{3,19},{4,0},{5,21},{6,2},{7,23},{8,12},{9,25},... | collective-permute-start | bytes 909320 | tf_op jit(solution)/shard_map/ppermute | solution.py:220
  19.4 8.4 %collective-permute-start.4 = (f32[592,128]{1,0:T(8,128)S(1)}, f32[592,128]{1,0:T(8,128)S(1)}, u32[]{:S(2)}, u32[]{:S(2)}) collective-permute-start(f32[592,128]{1,0:T(8,128)S(1)} %get-tuple-element.33), channel_id=1, source_target_pairs={{0,6},{1,25},{2,4},{3,27},{4,2},{5,29},{6,0},{7,31},{8,14},{9,17},... | collective-permute-start | bytes 909320 | tf_op jit(solution)/shard_map/ppermute | solution.py:220
  20.5 7.5 %collective-permute-start.6 = (f32[592,128]{1,0:T(8,128)S(1)}, f32[592,128]{1,0:T(8,128)S(1)}, u32[]{:S(2)}, u32[]{:S(2)}) collective-permute-start(f32[592,128]{1,0:T(8,128)S(1)} %get-tuple-element.34), channel_id=1, source_target_pairs={{0,2},{1,9},{2,0},{3,11},{4,6},{5,13},{6,4},{7,15},{8,10},{9,1},{1... | collective-permute-start | bytes 909320 | tf_op jit(solution)/shard_map/ppermute | solution.py:220
  20.5 1.5 %collective-permute-start = (f32[512,128]{1,0:T(8,128)S(1)}, f32[512,128]{1,0:T(8,128)S(1)}, u32[]{:S(2)}, u32[]{:S(2)}) collective-permute-start(f32[512,128]{1,0:T(8,128)S(1)} %bitcast.20), channel_id=1, source_target_pairs={{0,1},{1,0},{2,3},{3,2},{4,5},{5,4},{6,7},{7,6},{8,9},{9,8},{10,11... | collective-permute-start | bytes 786440 | tf_op jit(solution)/shard_map/ppermute | solution.py:210
  28.2 6.3 %collective-permute-start.7 = (f32[208,128]{1,0:T(8,128)S(1)}, f32[208,128]{1,0:T(8,128)S(1)}, u32[]{:S(2)}, u32[]{:S(2)}) collective-permute-start(f32[208,128]{1,0:T(8,128)S(1)} %get-tuple-element.29), channel_id=1, source_target_pairs={{0,64},{1,5},{2,66},{3,7},{4,68},{5,1},{6,70},{7,3},{8,72},{9,13},... | collective-permute-start | bytes 319496 | tf_op jit(solution)/shard_map/ppermute | solution.py:220
  31.5 5.9 %collective-permute-start.8 = (f32[208,128]{1,0:T(8,128)S(1)}, f32[208,128]{1,0:T(8,128)S(1)}, u32[]{:S(2)}, u32[]{:S(2)}) collective-permute-start(f32[208,128]{1,0:T(8,128)S(1)} %get-tuple-element.30), channel_id=1, source_target_pairs={{0,96},{1,7},{2,98},{3,5},{4,100},{5,3},{6,102},{7,1},{8,104},{9,1... | collective-permute-start | bytes 319496 | tf_op jit(solution)/shard_map/ppermute | solution.py:220
  32.5 4.9 %collective-permute-start.9 = (f32[208,128]{1,0:T(8,128)S(1)}, f32[208,128]{1,0:T(8,128)S(1)}, u32[]{:S(2)}, u32[]{:S(2)}) collective-permute-start(f32[208,128]{1,0:T(8,128)S(1)} %get-tuple-element.31), channel_id=1, source_target_pairs={{0,32},{1,3},{2,34},{3,1},{4,36},{5,7},{6,38},{7,5},{8,40},{9,11},... | collective-permute-start | bytes 319496 | tf_op jit(solution)/shard_map/ppermute | solution.py:220
  37.5 6.1 %collective-permute-start.12 = (f32[112,128]{1,0:T(8,128)S(1)}, f32[112,128]{1,0:T(8,128)S(1)}, u32[]{:S(2)}, u32[]{:S(2)}) collective-permute-start(f32[112,128]{1,0:T(8,128)S(1)} %get-tuple-element.26), channel_id=1, source_target_pairs={{0,16},{1,65},{2,18},{3,67},{4,20},{5,69},{6,22},{7,71},{8,24},{9,... | collective-permute-start | bytes 172040 | tf_op jit(solution)/shard_map/ppermute | solution.py:220
  41.4 4.2 %collective-permute-start.11 = (f32[112,128]{1,0:T(8,128)S(1)}, f32[112,128]{1,0:T(8,128)S(1)}, u32[]{:S(2)}, u32[]{:S(2)}) collective-permute-start(f32[112,128]{1,0:T(8,128)S(1)} %get-tuple-element.27), channel_id=1, source_target_pairs={{0,8},{1,33},{2,10},{3,35},{4,12},{5,37},{6,14},{7,39},{8,0},{9,41... | collective-permute-start | bytes 172040 | tf_op jit(solution)/shard_map/ppermute | solution.py:220
  42.5 5.4 %collective-permute-start.10 = (f32[112,128]{1,0:T(8,128)S(1)}, f32[112,128]{1,0:T(8,128)S(1)}, u32[]{:S(2)}, u32[]{:S(2)}) collective-permute-start(f32[112,128]{1,0:T(8,128)S(1)} %get-tuple-element.28), channel_id=1, source_target_pairs={{0,24},{1,97},{2,26},{3,99},{4,28},{5,101},{6,30},{7,103},{8,16},{... | collective-permute-start | bytes 172040 | tf_op jit(solution)/shard_map/ppermute | solution.py:220
